TPU v7x, 128 devices: a whole 4x4x4 slice. The times are simulated.
128 devices in a mesh: section: 2 (over core), expert: 16 (over y, z), head: 4 (over x).
Axes of the slice: x: 4, y: 4, z: 4, core: 2. Of those that a mesh axis runs over, the one named last changes fastest.
Arguments:
- boundary: bfloat16 [2, 2, 2048, 768], P('section', None, 'expert'), may hold values from -6 to 6
- segments: int32 [2, 16, 128], P(None, 'expert'), may hold values from 0 to 2, never falling along the last dimension, each value on 1 to 64 neighbouring positions
- buckets: int32 [128], replicated, may hold values from 0 to 31, as said below
- routes: int32 [2, 2, 2048, 2], P('section', None, 'expert'), may hold values from 0 to 15, as said below
- slots: int32 [2, 2, 2048, 2], P('section', None, 'expert'), may hold values from 0 to 29, as said below
- gains: float32 [2, 2, 768], P('section'), may hold values from 0.25 to 1.75
- qkv_weight: bfloat16 [2, 768, 3, 768], P('section', None, None, 'head'), may hold values from -4 to 4
- mix_weight: bfloat16 [2, 768, 768], P('section', 'head'), may hold values from -4 to 4
- bias_table: float32 [2, 32, 12], P('section', None, 'head'), may hold values from -3 to 3
- router: bfloat16 [2, 768, 16], P('section'), may hold values from -4 to 4
- expert_in: bfloat16 [2, 16, 768, 3072], P('section', 'expert', None, 'head'), may hold values from -4 to 4
- expert_out: bfloat16 [2, 16, 3072, 768], P('section', 'expert', 'head'), may hold values from -4 to 4
Outputs:
- boundary_out: bfloat16 [2, 2, 2048, 768], P('section', None, 'expert')
- grad_gains: float32 [2, 2, 768], P('section')
- grad_qkv: float32 [2, 768, 3, 768], P('section', None, None, 'head')
- grad_mix: float32 [2, 768, 768], P('section', 'head')
- grad_bias: float32 [2, 32, 12], P('section', None, 'head')
- grad_router: float32 [2, 768, 16], P('section')
- grad_expert_in: float32 [2, 16, 768, 3072], P('section', 'expert', None, 'head')
- grad_expert_out: float32 [2, 16, 3072, 768], P('section', 'expert', 'head')
Inputs may be any that keep to these rules, and one draw needn't show every extreme that they name: `routes`: each token names 2 different experts. For each layer and micro-batch one expert is named exactly 20 + 20 // 2 times by the tokens of every sequence; every other expert at most 20 times by the tokens of one sequence. The slots of the routes of one sequence to one expert are 0 up to their count minus one, each once. `buckets`: never falling with the distance; 0 at distance 0 and 31 at distance 128 - 1. `segments`: never falling along a sequence.
All inputs are finite; a program needn't handle non-finite values.
Results may differ from a plain program's by a relative error of at most 0.02.
Values may be sent and summed in bfloat16 or wider, within the bound.
A program may use at most 128 MiB of HBM per device.

v0:
```python
import jax
import jax.numpy as jnp
from jax import lax
from jax.sharding import PartitionSpec as P

HEAD_DIM = 64


EPSILON = 1e-06
NEGATIVE = -1e30
HIGHEST = lax.Precision.HIGHEST


def shifted(value, axis, steps):
    count = lax.axis_size(axis)
    first, last = (max(0, -steps), min(count, count - steps))
    return lax.ppermute(value, axis, [(source, source + steps) for source in range(first, last)])


def gelu_tanh(values):
    return (
        0.5
        * values
        * (1.0 + jnp.tanh(0.7978845608028654 * (values + 0.044715 * values * values * values)))
    )


def norm_forward(hidden, gain_row):
    row_scale = lax.rsqrt(jnp.mean(hidden * hidden, axis=-1, keepdims=True) + EPSILON)
    return (hidden * row_scale * gain_row, row_scale)


def norm_backward(grad_normed, hidden, row_scale, gain_row):
    unit_rows = hidden * row_scale
    grad_unit = grad_normed * gain_row
    grad_gain = jnp.sum(grad_normed * unit_rows, axis=0)
    grad_rows = row_scale * (
        grad_unit - unit_rows * jnp.mean(grad_unit * unit_rows, axis=-1, keepdims=True)
    )
    return (grad_rows, grad_gain)


def mixer_total(partial_value):
    return lax.psum(partial_value, "head")


def pass_forward(leaving):
    return shifted(leaving, "section", 1)


def pass_back(leaving):
    return shifted(leaving, "section", -1)


def to_owner(buffer):
    return lax.all_to_all(buffer, "expert", split_axis=0, concat_axis=0, tiled=True)


def to_source(partial_value, sources, capacity):
    summed = lax.psum(partial_value, "head").astype(jnp.bfloat16)
    return lax.all_to_all(
        summed.reshape(sources, capacity, -1), "expert", split_axis=0, concat_axis=0, tiled=True
    )


def contract_rows(left, right, precise=None):
    return lax.dot_general(
        left, right, (((0,), (0,)), ((), ())), precision=precise, preferred_element_type=jnp.float32
    )


def on_device(
    boundary,
    segments,
    buckets,
    routes,
    slots,
    gains,
    qkv_weight,
    mix_weight,
    bias_table,
    router,
    expert_in,
    expert_out,
):
    section_index = lax.axis_index("section")
    micro_count = boundary.shape[1]
    seq_len = boundary.shape[2]
    model_width = boundary.shape[3]
    experts = router.shape[2]
    route_count = routes.shape[3]
    sources = lax.axis_size("expert")
    capacity = 5 * route_count * seq_len // (4 * experts)
    local_heads = mix_weight.shape[1] // HEAD_DIM
    score_scale = HEAD_DIM ** (-0.5)
    gain_pair = gains[0]
    qkv_local = qkv_weight[0]
    mix_local = mix_weight[0]
    table_local = bias_table[0]
    router_local = router[0]
    inner_weight = expert_in[0, 0]
    outer_weight = expert_out[0, 0]
    my_routes = routes[0]
    my_slots = slots[0]
    my_segments = segments[:, 0]
    bucket_count = table_local.shape[0]
    position = jnp.arange(seq_len)
    distance = jnp.maximum(position[:, None] - position[None, :], 0)
    causal = position[None, :] <= position[:, None]
    pair_bucket = buckets[distance]
    pair_hot = (pair_bucket[:, :, None] == jnp.arange(bucket_count)[None, None, :]).astype(
        jnp.float32
    )
    bias_grid = jnp.einsum("qku,uh->hqk", pair_hot, table_local, precision=HIGHEST)
    slot_total = experts * capacity
    slot_ids = jnp.arange(slot_total, dtype=jnp.int32)
    expert_ids = jnp.arange(experts, dtype=jnp.int32)

    def attention_scores(queries, key_rows, allowed):
        scores = (
            jnp.einsum("qhd,khd->hqk", queries, key_rows, preferred_element_type=jnp.float32)
            * score_scale
        )
        return jnp.where(allowed[None], scores + bias_grid, NEGATIVE)

    zero_rows = jnp.zeros((seq_len, model_width), jnp.float32)
    arriving = zero_rows
    kept_states = []
    forward_outs = []
    for moment in range(micro_count + 1):
        micro_index = jnp.clip(moment - section_index, 0, micro_count - 1)
        if moment < micro_count:
            fresh_rows = boundary[0, moment].astype(jnp.float32)
        else:
            fresh_rows = zero_rows
        entering = jnp.where(section_index == 0, fresh_rows, arriving)
        segment_row = my_segments[micro_index]
        forward_allowed = causal & (segment_row[None, :] == segment_row[:, None])
        route_row = my_routes[micro_index]
        slot_row = my_slots[micro_index]
        forward_normed, forward_first_scale = norm_forward(entering, gain_pair[0])
        forward_normed = forward_normed.astype(jnp.bfloat16)
        projected = jnp.einsum(
            "td,dch->cth", forward_normed, qkv_local, preferred_element_type=jnp.float32
        ).astype(jnp.bfloat16)
        forward_queries = projected[0].reshape(seq_len, local_heads, HEAD_DIM)
        forward_key_rows = projected[1].reshape(seq_len, local_heads, HEAD_DIM)
        forward_value_rows = projected[2].reshape(seq_len, local_heads, HEAD_DIM)
        forward_scores = attention_scores(forward_queries, forward_key_rows, forward_allowed)
        top_score = jnp.max(forward_scores, axis=-1, keepdims=True)
        exp_scores = jnp.exp(forward_scores - top_score)
        row_total = jnp.sum(exp_scores, axis=-1, keepdims=True)
        forward_weights = exp_scores / row_total
        forward_log_total = top_score + jnp.log(row_total)
        forward_head_mix = jnp.einsum(
            "hqk,khd->qhd",
            forward_weights.astype(jnp.bfloat16),
            forward_value_rows,
            preferred_element_type=jnp.float32,
        )
        forward_head_mix = forward_head_mix.astype(jnp.bfloat16).reshape(seq_len, -1)
        forward_middle = entering + mixer_total(
            jnp.dot(forward_head_mix, mix_local, preferred_element_type=jnp.float32)
        )
        forward_normed_two, forward_second_scale = norm_forward(forward_middle, gain_pair[1])
        forward_normed_two = forward_normed_two.astype(jnp.bfloat16)
        logits = jnp.dot(forward_normed_two, router_local, preferred_element_type=jnp.float32)
        forward_expert_probs = jax.nn.softmax(logits, axis=-1)
        forward_expert_hot = (route_row[:, :, None] == expert_ids[None, None, :]).astype(
            jnp.float32
        )
        forward_gate_weights = jnp.sum(
            forward_expert_hot * forward_expert_probs[:, None, :], axis=-1
        )
        slot_index = jnp.where(slot_row < capacity, route_row * capacity + slot_row, slot_total)
        forward_route_hot = (slot_index.T[:, None, :] == slot_ids[None, :, None]).astype(
            jnp.bfloat16
        )
        outgoing = jnp.einsum(
            "kst,td->sd", forward_route_hot, forward_normed_two, preferred_element_type=jnp.float32
        )
        outgoing = outgoing.astype(jnp.bfloat16).reshape(experts, capacity, model_width)
        forward_arrived = to_owner(outgoing).reshape(sources * capacity, model_width)
        forward_pre_act = jnp.dot(forward_arrived, inner_weight, preferred_element_type=jnp.float32)
        forward_activated = gelu_tanh(forward_pre_act).astype(jnp.bfloat16)
        partial_value = jnp.dot(forward_activated, outer_weight, preferred_element_type=jnp.float32)
        returned = to_source(partial_value, sources, capacity).reshape(slot_total, model_width)
        forward_picked = jnp.einsum(
            "kst,sd->tkd", forward_route_hot, returned, preferred_element_type=jnp.float32
        )
        output = forward_middle + jnp.sum(forward_gate_weights[:, :, None] * forward_picked, axis=1)
        forward_layer_state = (
            entering,
            forward_normed,
            forward_first_scale,
            forward_queries,
            forward_key_rows,
            forward_value_rows,
            forward_log_total,
            forward_head_mix,
            forward_middle,
            forward_normed_two,
            forward_second_scale,
            forward_expert_probs,
            forward_gate_weights,
            forward_route_hot,
            forward_expert_hot,
            forward_allowed,
            forward_arrived,
            forward_pre_act,
            forward_activated,
            forward_picked,
        )
        leaving = output
        leaving = leaving.astype(jnp.bfloat16)
        kept_states.append(forward_layer_state)
        forward_outs.append(leaving)
        if moment < micro_count:
            arriving = pass_forward(leaving).astype(jnp.float32)
    arriving = zero_rows
    backward_outs = []
    totals = None
    expert_totals = None
    for moment in range(micro_count + 1):
        index_now = micro_count - 1 - moment + (1 - section_index)
        is_valid = (index_now >= 0) & (index_now < micro_count)
        if moment < micro_count:
            fresh_rows = boundary[0, micro_count - 1 - moment].astype(jnp.float32)
        else:
            fresh_rows = zero_rows
        entering = jnp.where(section_index == 1, fresh_rows, arriving)
        (
            hidden,
            normed,
            first_scale,
            backward_queries,
            backward_key_rows,
            value_rows,
            log_total,
            head_mix,
            middle,
            normed_two,
            second_scale,
            expert_probs,
            gate_weights,
            route_hot,
            expert_hot,
            backward_allowed,
            arrived,
            pre_act,
            activated,
            picked,
        ) = kept_states[micro_count - moment]
        grad_gate = jnp.sum(entering[:, None, :] * picked, axis=-1)
        grad_copies = (gate_weights[:, :, None] * entering[:, None, :]).astype(jnp.bfloat16)
        grad_buffer = jnp.einsum(
            "kst,tkd->sd", route_hot, grad_copies, preferred_element_type=jnp.float32
        )
        grad_buffer = grad_buffer.astype(jnp.bfloat16).reshape(experts, capacity, model_width)
        grad_arrived = to_owner(grad_buffer).reshape(sources * capacity, model_width)
        grad_act = jnp.dot(grad_arrived, outer_weight.T, preferred_element_type=jnp.float32)
        gelu_values, gelu_pull = jax.vjp(gelu_tanh, pre_act)
        grad_pre = gelu_pull(grad_act)[0].astype(jnp.bfloat16)
        backward_grad_outer = contract_rows(activated, grad_arrived)
        backward_grad_inner = contract_rows(arrived, grad_pre)
        grad_in_part = jnp.dot(grad_pre, inner_weight.T, preferred_element_type=jnp.float32)
        back_rows = to_source(grad_in_part, sources, capacity).reshape(slot_total, model_width)
        grad_normed_two = jnp.einsum(
            "kst,sd->td", route_hot, back_rows, preferred_element_type=jnp.float32
        )
        grad_probs = jnp.sum(grad_gate[:, :, None] * expert_hot, axis=1)
        grad_logits = expert_probs * (
            grad_probs - jnp.sum(expert_probs * grad_probs, axis=-1, keepdims=True)
        )
        grad_logits = grad_logits.astype(jnp.bfloat16)
        backward_grad_router = contract_rows(normed_two, grad_logits)
        grad_normed_two = grad_normed_two + jnp.dot(
            grad_logits, router_local.T, preferred_element_type=jnp.float32
        )
        grad_middle_norm, grad_gain_two = norm_backward(
            grad_normed_two, middle, second_scale, gain_pair[1]
        )
        grad_middle = entering + grad_middle_norm
        grad_attn = grad_middle.astype(jnp.bfloat16)
        backward_grad_mix = contract_rows(head_mix, grad_attn)
        grad_head_mix = jnp.dot(grad_attn, mix_local.T, preferred_element_type=jnp.float32).astype(
            jnp.bfloat16
        )
        grad_head_mix = grad_head_mix.reshape(seq_len, local_heads, HEAD_DIM)
        backward_scores = attention_scores(backward_queries, backward_key_rows, backward_allowed)
        weights = jnp.exp(backward_scores - log_total)
        grad_weights = jnp.einsum(
            "qhd,khd->hqk", grad_head_mix, value_rows, preferred_element_type=jnp.float32
        )
        grad_scores = weights * (
            grad_weights - jnp.sum(weights * grad_weights, axis=-1, keepdims=True)
        )
        backward_grad_table = jnp.einsum("hqk,qku->uh", grad_scores, pair_hot, precision=HIGHEST)
        scores_low = grad_scores.astype(jnp.bfloat16)
        grad_queries = (
            jnp.einsum(
                "hqk,khd->qhd", scores_low, backward_key_rows, preferred_element_type=jnp.float32
            )
            * score_scale
        )
        grad_keys = (
            jnp.einsum(
                "hqk,qhd->khd", scores_low, backward_queries, preferred_element_type=jnp.float32
            )
            * score_scale
        )
        grad_values = jnp.einsum(
            "hqk,qhd->khd",
            weights.astype(jnp.bfloat16),
            grad_head_mix,
            preferred_element_type=jnp.float32,
        )
        grad_project = (
            jnp.stack([grad_queries, grad_keys, grad_values])
            .reshape(3, seq_len, -1)
            .astype(jnp.bfloat16)
        )
        backward_grad_qkv = jnp.einsum(
            "td,cth->dch", normed, grad_project, preferred_element_type=jnp.float32
        )
        grad_normed = mixer_total(
            jnp.einsum("cth,dch->td", grad_project, qkv_local, preferred_element_type=jnp.float32)
        )
        grad_hidden_norm, grad_gain_one = norm_backward(
            grad_normed, hidden, first_scale, gain_pair[0]
        )
        grad_hidden = grad_middle + grad_hidden_norm
        shared = (
            jnp.stack([grad_gain_one, grad_gain_two]),
            backward_grad_qkv,
            backward_grad_mix,
            backward_grad_table,
            backward_grad_router,
        )
        grad_hidden, shared, expert_grads = (
            grad_hidden,
            shared,
            (backward_grad_inner, backward_grad_outer),
        )
        shared = jax.tree.map(lambda element: jnp.where(is_valid, element, 0.0), shared)
        expert_grads = jax.tree.map(lambda element: jnp.where(is_valid, element, 0.0), expert_grads)
        if totals is None:
            totals = shared
            expert_totals = expert_grads
        else:
            totals = jax.tree.map(jnp.add, totals, shared)
            expert_totals = jax.tree.map(jnp.add, expert_totals, expert_grads)
        leaving = grad_hidden.astype(jnp.bfloat16)
        backward_outs.append(leaving)
        if moment < micro_count:
            arriving = pass_back(leaving).astype(jnp.float32)
    totals = lax.psum(totals, "expert")
    rows_out = [
        jnp.where(
            section_index == 1,
            forward_outs[micro_slot + 1],
            backward_outs[micro_count - micro_slot],
        )
        for micro_slot in range(micro_count)
    ]
    boundary_out = jnp.stack(rows_out)[None]
    grad_gains, grad_qkv, grad_mix, grad_table, grad_router = totals
    grad_inner, grad_outer = expert_totals
    return (
        boundary_out,
        grad_gains[None],
        grad_qkv[None],
        grad_mix[None],
        grad_table[None],
        grad_router[None],
        grad_inner[None, None],
        grad_outer[None, None],
    )


def solution(mesh):
    in_specs = (
        P("section", None, "expert", None),
        P(None, "expert", None),
        P(),
        P("section", None, "expert", None),
        P("section", None, "expert", None),
        P("section", None, None),
        P("section", None, None, "head"),
        P("section", "head", None),
        P("section", None, "head"),
        P("section", None, None),
        P("section", "expert", None, "head"),
        P("section", "expert", "head", None),
    )
    out_specs = (
        P("section", None, "expert", None),
        P("section", None, None),
        P("section", None, None, "head"),
        P("section", "head", None),
        P("section", None, "head"),
        P("section", None, None),
        P("section", "expert", None, "head"),
        P("section", "expert", "head", None),
    )
    return jax.shard_map(
        on_device, mesh=mesh, in_specs=in_specs, out_specs=out_specs, check_vma=False
    )
```

profile of v0, /device:TPU:0, one launch (start us, length us, event | category | flops | bytes accessed | tf_op | source)
XLA Modules:
  0.0 949.1 jit_solution(5039355712128968961)
XLA Ops:
  10.6 97.2 %gather_fusion = s32[16384]{0:T(1024)S(1)} fusion(s32[128]{0:T(128)S(1)} %copy-done.1, s32[16384]{0:T(1024)S(1)} %bitcast_clamp_fusion), kind=kCustom, calls=%fused_computation | custom fusion | bytes 196608 | tf_op jit(solution)/shard_map/gather | solution.py:110
  112.2 43.4 %all-reduce.16.cloned.1.call-done = f32[128,768]{1,0:T(8,128)} async-done(((f32[128,768]{1,0:T(8,128)}), f32[128,768]{1,0:T(8,128)}) %all-reduce.16.cloned.1.call-update) | async-done | bytes 393232 | tf_op jit(solution)/shard_map/psum | solution.py:44
  158.7 2.0 reshape.469
  160.7 17.6 %all_to_all.60 = bf16[16,20,768]{2,1,0:T(8,128)(2,1)} all-to-all(bf16[16,20,768]{2,1,0:T(8,128)(2,1)} %reshape.469), channel_id=1, replica_groups=mesh['section'=2,'expert'=16,'head'=4] {'expert'}, dimensions={0} | all-to-all | bytes 983040 | tf_op jit(solution)/shard_map/all_to_all | solution.py:56
  184.5 27.6 %all-reduce.29 = bf16[320,768]{1,0:T(8,128)(2,1)} all-reduce(f32[320,768]{1,0:T(8,128)} %fusion.20), channel_id=1, replica_groups=mesh['section'=2,'expert'=16,'head'=4] {'head'}, use_global_device_ids=true, to_apply=%region_9.10 | all-reduce | flops 245760 | bytes 1474560 | tf_op jit(solution)/shard_map/psum | solution.py:60
  214.0 4.3 all-to-all-start.1
  221.8 6.9 all-to-all-done.1
  230.6 3.1 multiply_reduce_fusion.5
  244.3 38.5 %all-reduce.18.cloned.1.call-done = f32[128,768]{1,0:T(8,128)} async-done(((f32[128,768]{1,0:T(8,128)}), f32[128,768]{1,0:T(8,128)}) %all-reduce.18.cloned.1.call-update) | async-done | bytes 393232 | tf_op jit(solution)/shard_map/psum | solution.py:44
  282.9 2.0 multiply_reduce_fusion.18
  289.5 17.6 %all_to_all.61 = bf16[16,20,768]{2,1,0:T(8,128)(2,1)} all-to-all(bf16[16,20,768]{2,1,0:T(8,128)(2,1)} %reshape.474), channel_id=1, replica_groups=mesh['section'=2,'expert'=16,'head'=4] {'expert'}, dimensions={0} | all-to-all | bytes 983040 | tf_op jit(solution)/shard_map/all_to_all | solution.py:56
  307.1 2.0 reshape.475
  313.3 27.5 %all-reduce.30 = bf16[320,768]{1,0:T(8,128)(2,1)} all-reduce(f32[320,768]{1,0:T(8,128)} %fusion.18), channel_id=1, replica_groups=mesh['section'=2,'expert'=16,'head'=4] {'head'}, use_global_device_ids=true, to_apply=%region_20.21 | all-reduce | flops 245760 | bytes 1474560 | tf_op jit(solution)/shard_map/psum | solution.py:60
  342.7 4.3 all-to-all-start.3
  350.6 6.8 all-to-all-done.3
  359.4 3.1 multiply_reduce_fusion.4
  374.1 35.3 %all-reduce.20.cloned.1.call-done = f32[128,768]{1,0:T(8,128)} async-done(((f32[128,768]{1,0:T(8,128)}), f32[128,768]{1,0:T(8,128)}) %all-reduce.20.cloned.1.call-update) | async-done | bytes 393232 | tf_op jit(solution)/shard_map/psum | solution.py:44
  411.5 2.1 fusion.242
  416.6 7.0 all-to-all-start.4
  427.0 2.1 fusion.4
  431.0 3.2 all-to-all-done.4
  434.2 4.3 all-to-all-start.5
  438.4 2.0 reshape.480
  444.6 4.3 all-to-all-done.5
  450.8 2.5 fusion.73
  455.6 39.2 %all-reduce.31 = (bf16[320,768]{1,0:T(8,128)(2,1)}, bf16[320,768]{1,0:T(8,128)(2,1)}) all-reduce(f32[320,768]{1,0:T(8,128)} %fusion.26, f32[320,768]{1,0:T(8,128)} %fusion.14), channel_id=1, replica_groups=mesh['section'=2,'expert'=16,'head'=4] {'head'}, use_global_device_ids=true, to_apply=%region_31.32 | all-reduce | flops 491520 | bytes 2949120 | tf_op jit(solution)/shard_map/psum | solution.py:60
  496.8 4.3 all-to-all-start.6
  506.8 4.8 all-to-all-done.6
  511.6 4.3 all-to-all-start.7
  515.9 3.6 fusion.227
  521.4 2.1 fusion.243
  523.6 2.7 all-to-all-done.7
  528.3 2.4 multiply_reduce_fusion
  536.0 3.4 fusion.246
  544.2 31.4 %all-reduce.22.cloned.1.call-done = f32[128,768]{1,0:T(8,128)} async-done(((f32[128,768]{1,0:T(8,128)}), f32[128,768]{1,0:T(8,128)}) %all-reduce.22.cloned.1.call-update) | async-done | bytes 393232 | tf_op jit(solution)/shard_map/psum | solution.py:44
  585.0 2.1 fusion.5
  589.1 7.3 all-to-all-start.8
  596.3 2.7 fusion.57
  599.0 2.7 fusion.186
  601.7 7.3 all-to-all-done.8
  610.9 2.5 fusion.69
  615.7 27.1 %all-reduce.32 = bf16[320,768]{1,0:T(8,128)(2,1)} all-reduce(f32[320,768]{1,0:T(8,128)} %fusion.24), channel_id=1, replica_groups=mesh['section'=2,'expert'=16,'head'=4] {'head'}, use_global_device_ids=true, to_apply=%region_40.41 | all-reduce | flops 245760 | bytes 1474560 | tf_op jit(solution)/shard_map/psum | solution.py:60
  644.7 4.7 all-to-all-start.9
  653.5 6.4 all-to-all-done.9
  663.3 2.0 multiply_reduce_fusion.7
  673.7 34.5 %all-reduce.24.cloned.1.call-done = f32[128,768]{1,0:T(8,128)} async-done(((f32[128,768]{1,0:T(8,128)}), f32[128,768]{1,0:T(8,128)}) %all-reduce.24.cloned.1.call-update) | async-done | bytes 393232 | tf_op jit(solution)/shard_map/psum | solution.py:44
  708.2 2.1 multiply_reduce_fusion.8
  710.3 2.4 fusion.135
  714.0 2.3 fusion.226
  719.7 2.1 fusion.6
  723.8 7.0 all-to-all-start.10
  730.9 2.4 fusion.8
  735.8 8.7 all-to-all-done.10
  746.4 2.5 fusion.65
  751.2 29.5 %all-reduce.33 = bf16[320,768]{1,0:T(8,128)(2,1)} all-reduce(f32[320,768]{1,0:T(8,128)} %fusion.22), channel_id=1, replica_groups=mesh['section'=2,'expert'=16,'head'=4] {'head'}, use_global_device_ids=true, to_apply=%region_48.49 | all-reduce | flops 245760 | bytes 1474560 | tf_op jit(solution)/shard_map/psum | solution.py:60
  782.7 4.4 all-to-all-start.11
  788.8 8.8 all-to-all-done.11
  807.8 2.0 fusion.247
  811.2 2.4 add_bitcast_fusion.1
  814.8 2.4 add_bitcast_fusion
  818.4 23.1 %all-reduce.26.cloned.1.call-done = f32[128,768]{1,0:T(8,128)} async-done(((f32[128,768]{1,0:T(8,128)}), f32[128,768]{1,0:T(8,128)}) %all-reduce.26.cloned.1.call-update) | async-done | bytes 393232 | tf_op jit(solution)/shard_map/psum | solution.py:44
  842.8 75.5 %all-reduce = (f32[1,2,768]{2,1,0:T(2,128)}, f32[1,32,3]{1,2,0:T(4,128)S(1)}, f32[1,768,16]{1,2,0:T(8,128)}) all-reduce(f32[1,2,768]{2,1,0:T(2,128)S(1)} %fusion.205, f32[1,32,3]{1,2,0:T(4,128)S(1)} %fusion.54, f32[1,768,16]{1,2,0:T(8,128)S(1)} %fusion.47), channel_id=1, replica_groups=mesh['section'=2,'expert'=16,'head'=4] {'expert'}, use_global_device_ids=true, to_apply=%region_63.64 | all-reduce | flops 13920 | bytes 111360 | tf_op jit(solution)/shard_map/psum | solution.py:357
  920.8 17.4 %all-reduce.28.cloned.1.call-done = (f32[1,768,3,192]{1,3,2,0:T(8,128)}, f32[1,192,768]{2,1,0:T(8,128)}) async-done(((f32[1,768,3,192]{1,3,2,0:T(8,128)}, f32[1,192,768]{2,1,0:T(8,128)}), (f32[1,768,3,192]{1,3,2,0:T(8,128)}, f32[1,192,768]{2,1,0:T(8,128)})) %all-reduce.28.cloned.1.call-update) | async-done | bytes 2359312 | tf_op jit(solution)/shard_map/psum | solution.py:357
  938.2 2.9 copy.198
  (498 shorter events, 171.1 us)
Async XLA Ops:
  7.2 175.6 %copy-start = (bf16[1,1,768,768]{3,2,1,0:T(8,128)(2,1)S(1)}, bf16[1,1,768,768]{3,2,1,0:T(8,128)(2,1)}, u32[]{:S(2)}) copy-start(bf16[1,1,768,768]{3,2,1,0:T(8,128)(2,1)} %param.23) | copy-start | bytes 3538948
  7.2 3.4 copy-start.1
  7.2 148.5 %all-reduce.16.cloned.1.call-start = ((), (), s32[]{:S(2)}) async-start(), calls=%async_computation.12 | async-start | bytes 786432 | tf_op jit(solution)/shard_map/psum | solution.py:44
  8.4 99.5 %copy-start.146 = (f32[128]{0:T(128)}, f32[128]{0:T(128)S(1)}, u32[]{:S(2)}) copy-start(f32[128]{0:T(128)S(1)} %add_rsqrt_fusion.5) | copy-start | bytes 1540
  10.6 97.4 %copy-start.3 = (bf16[1,768,3,192]{1,3,2,0:T(8,128)(2,1)S(1)}, bf16[1,768,3,192]{1,3,2,0:T(8,128)(2,1)}, u32[]{:S(2)}) copy-start(bf16[1,768,3,192]{1,3,2,0:T(8,128)(2,1)} %param.18) | copy-start | bytes 2654212
  10.6 97.4 %copy-start.4 = (bf16[1,2,128,768]{3,2,1,0:T(8,128)(2,1)S(1)}, bf16[1,2,128,768]{3,2,1,0:T(8,128)(2,1)}, u32[]{:S(2)}) copy-start(bf16[1,2,128,768]{3,2,1,0:T(8,128)(2,1)} %param.12) | copy-start | bytes 1179652
  108.6 48.2 %copy-start.97 = (bf16[1,128,192]{1,2,0:T(8,128)(2,1)}, bf16[1,128,192]{1,2,0:T(8,128)(2,1)S(1)}, u32[]{:S(2)}) copy-start(bf16[1,128,192]{1,2,0:T(8,128)(2,1)S(1)} %get-tuple-element.86) | copy-start | bytes 147460
  109.6 47.4 %copy-start.112 = (f32[3,128]{1,0:T(4,128)}, f32[3,128]{1,0:T(4,128)S(1)}, u32[]{:S(2)}) copy-start(f32[3,128]{1,0:T(4,128)S(1)} %get-tuple-element.94) | copy-start | bytes 4612
  109.8 47.1 %copy-start.91 = (bf16[3,64,128]{2,1,0:T(8,128)(2,1)}, bf16[3,64,128]{2,1,0:T(8,128)(2,1)S(1)}, u32[]{:S(2)}) copy-start(bf16[3,64,128]{2,1,0:T(8,128)(2,1)S(1)} %convolution_convert_fusion.8) | copy-start | bytes 147460
  111.5 45.5 %copy-start.117 = (s32[2,128]{1,0:T(2,128)}, s32[2,128]{1,0:T(2,128)S(1)}, u32[]{:S(2)}) copy-start(s32[2,128]{1,0:T(2,128)S(1)} %get-tuple-element.87) | copy-start | bytes 3076
  111.5 45.5 %copy-start.118 = (s32[2,128]{1,0:T(2,128)}, s32[2,128]{1,0:T(2,128)S(1)}, u32[]{:S(2)}) copy-start(s32[2,128]{1,0:T(2,128)S(1)} %get-tuple-element.89) | copy-start | bytes 3076
  112.2 44.8 %copy-start.65 = (bf16[320,128]{1,0:T(8,128)(2,1)}, bf16[320,128]{1,0:T(8,128)(2,1)S(1)}, u32[]{:S(2)}) copy-start(bf16[320,128]{1,0:T(8,128)(2,1)S(1)} %get-tuple-element.122) | copy-start | bytes 245764
  158.7 21.6 %copy-start.2 = (bf16[1,1,768,768]{3,2,1,0:T(8,128)(2,1)S(1)}, bf16[1,1,768,768]{3,2,1,0:T(8,128)(2,1)}, u32[]{:S(2)}) copy-start(bf16[1,1,768,768]{3,2,1,0:T(8,128)(2,1)} %param.22) | copy-start | bytes 3538948
  214.0 14.7 %all-to-all-start.1 = ((bf16[16,20,768]{2,1,0:T(8,128)(2,1)}), bf16[16,20,768]{2,1,0:T(8,128)(2,1)}, u32[]{:S(2)}, u32[]{:S(2)}) async-start(bf16[16,20,768]{2,1,0:T(8,128)(2,1)} %reshape.471), calls=%async_computation.1 | async-start | bytes 1179648 | tf_op jit(solution)/shard_map/all_to_all | solution.py:61
  218.2 64.7 %all-reduce.18.cloned.1.call-start = ((), (), s32[]{:S(2)}) async-start(), calls=%async_computation.13 | async-start | bytes 786432 | tf_op jit(solution)/shard_map/psum | solution.py:44
  235.6 6.6 copy-start.54
  236.8 2.7 collective-permute-start
  282.9 3.6 copy-start.67
  342.7 14.7 %all-to-all-start.3 = ((bf16[16,20,768]{2,1,0:T(8,128)(2,1)}), bf16[16,20,768]{2,1,0:T(8,128)(2,1)}, u32[]{:S(2)}, u32[]{:S(2)}) async-start(bf16[16,20,768]{2,1,0:T(8,128)(2,1)} %reshape.476), calls=%async_computation.3 | async-start | bytes 1179648 | tf_op jit(solution)/shard_map/all_to_all | solution.py:61
  347.0 62.4 %all-reduce.20.cloned.1.call-start = ((), (), s32[]{:S(2)}) async-start(), calls=%async_computation.14 | async-start | bytes 786432 | tf_op jit(solution)/shard_map/psum | solution.py:44
  364.4 4.3 copy-start.55
  364.4 4.3 copy-start.103
  365.6 2.4 collective-permute-start.1
  409.4 4.2 copy-start.68
  416.6 17.5 %all-to-all-start.4 = ((bf16[16,20,768]{2,1,0:T(8,128)(2,1)}), bf16[16,20,768]{2,1,0:T(8,128)(2,1)}, u32[]{:S(2)}, u32[]{:S(2)}) async-start(bf16[16,20,768]{2,1,0:T(8,128)(2,1)} %reshape.479), calls=%async_computation.4 | async-start | bytes 1179648 | tf_op jit(solution)/shard_map/all_to_all | solution.py:56
  434.2 14.7 %all-to-all-start.5 = ((bf16[16,20,768]{2,1,0:T(8,128)(2,1)}), bf16[16,20,768]{2,1,0:T(8,128)(2,1)}, u32[]{:S(2)}, u32[]{:S(2)}) async-start(bf16[16,20,768]{2,1,0:T(8,128)(2,1)} %reshape.481), calls=%async_computation.5 | async-start | bytes 1179648 | tf_op jit(solution)/shard_map/all_to_all | solution.py:56
  496.8 14.8 %all-to-all-start.6 = ((bf16[16,20,768]{2,1,0:T(8,128)(2,1)}), bf16[16,20,768]{2,1,0:T(8,128)(2,1)}, u32[]{:S(2)}, u32[]{:S(2)}) async-start(bf16[16,20,768]{2,1,0:T(8,128)(2,1)} %reshape.483), calls=%async_computation.6 | async-start | bytes 1179648 | tf_op jit(solution)/shard_map/all_to_all | solution.py:61
  511.6 14.7 %all-to-all-start.7 = ((bf16[16,20,768]{2,1,0:T(8,128)(2,1)}), bf16[16,20,768]{2,1,0:T(8,128)(2,1)}, u32[]{:S(2)}, u32[]{:S(2)}) async-start(bf16[16,20,768]{2,1,0:T(8,128)(2,1)} %reshape.485), calls=%async_computation.7 | async-start | bytes 1179648 | tf_op jit(solution)/shard_map/all_to_all | solution.py:61
  515.8 59.7 %all-reduce.22.cloned.1.call-start = ((), (), s32[]{:S(2)}) async-start(), calls=%async_computation.15 | async-start | bytes 786432 | tf_op jit(solution)/shard_map/psum | solution.py:44
  528.3 3.5 copy-start.5
  575.5 4.7 copy-start.23
  575.6 4.7 copy-start.95
  575.6 6.7 copy-start.6
  579.0 3.3 collective-permute-start.2
  589.1 19.9 %all-to-all-start.8 = ((bf16[16,20,768]{2,1,0:T(8,128)(2,1)}), bf16[16,20,768]{2,1,0:T(8,128)(2,1)}, u32[]{:S(2)}, u32[]{:S(2)}) async-start(bf16[16,20,768]{2,1,0:T(8,128)(2,1)} %reshape.488), calls=%async_computation.8 | async-start | bytes 1179648 | tf_op jit(solution)/shard_map/all_to_all | solution.py:56
  644.7 15.2 %all-to-all-start.9 = ((bf16[16,20,768]{2,1,0:T(8,128)(2,1)}), bf16[16,20,768]{2,1,0:T(8,128)(2,1)}, u32[]{:S(2)}, u32[]{:S(2)}) async-start(bf16[16,20,768]{2,1,0:T(8,128)(2,1)} %reshape.490), calls=%async_computation.9 | async-start | bytes 1179648 | tf_op jit(solution)/shard_map/all_to_all | solution.py:61
  649.3 58.9 %all-reduce.24.cloned.1.call-start = ((), (), s32[]{:S(2)}) async-start(), calls=%async_computation.16 | async-start | bytes 786432 | tf_op jit(solution)/shard_map/psum | solution.py:44
  661.8 3.5 copy-start.13
  661.8 3.5 copy-start.36
  661.8 3.5 copy-start.143
  663.2 3.5 copy-start.100
  708.2 5.7 copy-start.57
  708.2 5.8 copy-start.70
  712.7 3.7 collective-permute-start.3
  723.8 20.6 %all-to-all-start.10 = ((bf16[16,20,768]{2,1,0:T(8,128)(2,1)}), bf16[16,20,768]{2,1,0:T(8,128)(2,1)}, u32[]{:S(2)}, u32[]{:S(2)}) async-start(bf16[16,20,768]{2,1,0:T(8,128)(2,1)} %reshape.493), calls=%async_computation.10 | async-start | bytes 1179648 | tf_op jit(solution)/shard_map/all_to_all | solution.py:56
  751.2 36.2 %copy-start.35 = (f32[128,768]{0,1:T(8,128)S(1)}, f32[128,768]{0,1:T(8,128)}, u32[]{:S(2)}) copy-start(f32[128,768]{0,1:T(8,128)} %copy.136) | copy-start | bytes 1179652
  780.8 7.9 copy-start.125
  780.8 8.0 copy-start.120
  780.8 8.0 copy-start.131
  782.7 16.0 %copy-start.66 = (bf16[320,128]{1,0:T(8,128)(2,1)S(1)}, bf16[320,128]{1,0:T(8,128)(2,1)}, u32[]{:S(2)}) copy-start(bf16[320,128]{1,0:T(8,128)(2,1)} %copy-done.65) | copy-start | bytes 245764
  782.7 14.9 %all-to-all-start.11 = ((bf16[16,20,768]{2,1,0:T(8,128)(2,1)}), bf16[16,20,768]{2,1,0:T(8,128)(2,1)}, u32[]{:S(2)}, u32[]{:S(2)}) async-start(bf16[16,20,768]{2,1,0:T(8,128)(2,1)} %reshape.495), calls=%async_computation.11 | async-start | bytes 1179648 | tf_op jit(solution)/shard_map/all_to_all | solution.py:61
  787.1 11.9 %copy-start.11 = (f32[128,768]{1,0:T(8,128)S(1)}, f32[128,768]{1,0:T(8,128)}, u32[]{:S(2)}) copy-start(f32[128,768]{1,0:T(8,128)} %copy-done.10) | copy-start | bytes 1179652
  787.1 11.9 %copy-start.60 = (bf16[1,768,16]{1,2,0:T(8,128)(2,1)S(1)}, bf16[1,768,16]{1,2,0:T(8,128)(2,1)}, u32[]{:S(2)}) copy-start(bf16[1,768,16]{1,2,0:T(8,128)(2,1)} %param.21) | copy-start | bytes 73732
  787.1 11.9 %copy-start.141 = (f32[128]{0:T(128)S(1)}, f32[128]{0:T(128)}, u32[]{:S(2)}) copy-start(f32[128]{0:T(128)} %copy-done.140) | copy-start | bytes 1540
  787.1 54.3 %all-reduce.26.cloned.1.call-start = ((), (), s32[]{:S(2)}) async-start(), calls=%async_computation.17 | async-start | bytes 786432 | tf_op jit(solution)/shard_map/psum | solution.py:44
  788.8 11.8 %copy-start.107 = (bf16[128,16]{0,1:T(8,128)(2,1)}, bf16[128,16]{0,1:T(8,128)(2,1)S(1)}, u32[]{:S(2)}) copy-start(bf16[128,16]{0,1:T(8,128)(2,1)S(1)} %multiply_convert_fusion.16) | copy-start | bytes 12292
  803.0 135.2 %all-reduce.28.cloned.1.call-start = ((), (), s32[]{:S(2)}) async-start(), calls=%async_computation.18 | async-start | bytes 4718592 | tf_op jit(solution)/shard_map/psum | solution.py:357
  807.8 3.4 copy-start.16
  811.2 3.6 copy-start.42
  811.2 3.6 copy-start.46
  814.8 27.9 %copy-start.123 = (f32[1,768]{1,0:T(1,128)S(1)}, f32[1,768]{1,0:T(1,128)}, u32[]{:S(2)}) copy-start(f32[1,768]{1,0:T(1,128)} %stack.88) | copy-start | bytes 9220
  814.8 27.9 %copy-start.124 = (f32[1,768]{1,0:T(1,128)S(1)}, f32[1,768]{1,0:T(1,128)}, u32[]{:S(2)}) copy-start(f32[1,768]{1,0:T(1,128)} %stack.87) | copy-start | bytes 9220
  814.8 104.0 %copy-start.63 = (bf16[128,768]{1,0:T(8,128)(2,1)S(1)}, bf16[128,768]{1,0:T(8,128)(2,1)}, u32[]{:S(2)}) copy-start(bf16[128,768]{1,0:T(8,128)(2,1)} %copy-done.62) | copy-start | bytes 589828
  817.2 102.8 %copy-start.64 = (bf16[1,128,768]{2,1,0:T(8,128)(2,1)S(1)}, bf16[1,128,768]{2,1,0:T(8,128)(2,1)}, u32[]{:S(2)}) copy-start(bf16[1,128,768]{2,1,0:T(8,128)(2,1)} %get-tuple-element.63) | copy-start | bytes 589828
  (108 other events, 179.9 us)
Sparse Core Ops, SparseCore 0:
  111.0 44.6 all-reduce.15
  244.5 38.3 all-reduce.17
  370.9 38.4 all-reduce.19
  536.2 39.3 all-reduce.21
  669.8 38.4 all-reduce.23
  803.1 38.3 all-reduce.25
  845.5 92.6 all-reduce.27
where the time goes:
time: 962 us; the launch traced here: 949 us
  waiting for transfers between devices  285 us (30%)
  blocking collectives  262 us (27%)
  local copies, waits for them, and re-layouts  184 us (19%)
  matrix products  98.1 us (10%)
  starting transfers between devices  57.5 us (6%)
  other arithmetic  46.1 us (5%)
  between operations  16.6 us (2%)
    psum x6, waiting for transfers between devices, mixer_total(): return lax.psum(partial_value, 'head')  206 us
    psum x5, blocking collectives, to_source(): summed = lax.psum(partial_value, 'head').astype(jnp.bfloat16)  151 us
    gather x2, local copies, waits for them, and re-layouts, on_device(): pair_bucket = buckets[distance]  97.3 us
    psum x1, blocking collectives, on_device(): totals = lax.psum(totals, 'expert')  75.5 us
    all_to_all x6, waiting for transfers between devices, to_source(): lax.all_to_all(summed.reshape(sources, capacity, -1), 'expert', split_axi...  36.3 us
    all_to_all x2, blocking collectives, to_owner(): lax.all_to_all(buffer, 'expert', split_axis=0, concat_axis=0, tiled=True)  35.1 us
    all_to_all x6, starting transfers between devices, to_source(): lax.all_to_all(summed.reshape(sources, capacity, -1), 'expert', split_axi...  26.1 us
    all_to_all x4, starting transfers between devices, to_owner(): lax.all_to_all(buffer, 'expert', split_axis=0, concat_axis=0, tiled=True)  25.6 us
  transfers between devices with their start and end apart: 21, of which 19 were waited for; matrix products, arithmetic and copies ran while one was open for 9% of the time, Pallas kernels for 0%

commit v1 on v0

v1 whole, which is shorter than its diff:
```python
import jax
import jax.numpy as jnp
from jax import lax
from jax.experimental import pallas as pl
from jax.experimental.pallas import tpu as pltpu
from jax.sharding import PartitionSpec as P

MESH = pl.DeviceIdType.MESH
EPS = 1e-06
NEG = -1e30
BF = jnp.bfloat16
F32 = jnp.float32
T = 128
D = 768
NE = 16
NX = 4
CAP = 20
TR = T // NX
SCALE = 0.125


def nn(a, b):
    return lax.dot_general(a, b, (((1,), (0,)), ((), ())), preferred_element_type=F32)


def nt(a, b):
    return lax.dot_general(a, b, (((1,), (1,)), ((), ())), preferred_element_type=F32)


def tn(a, b):
    return lax.dot_general(a, b, (((0,), (0,)), ((), ())), preferred_element_type=F32)


def iota(shape, dim):
    return lax.broadcasted_iota(jnp.int32, shape, dim)


def row_roll(x, right):
    rows = iota((T, T), 0)
    for bit in range(7):
        step = 1 << bit
        turned = pltpu.roll(x, step if right else T - step, 1)
        x = jnp.where((rows >> bit) & 1 == 1, turned, x)
    return x


SEMS = {}


def sem_id(name):
    return SEMS.setdefault(name, len(SEMS))


SCRATCH = dict(
    HB=((2, T, D), BF),
    HX=((T, D), BF),
    SEG=((2, 1, T), jnp.int32),
    BK=((1, T), jnp.int32),
    RO=((2, 2, T), jnp.int32),
    SL=((2, 2, T), jnp.int32),
    GN=((2, 2, D), F32),
    TB=((2, 3, 32), F32),
    RT=((2, NE, D), BF),
    QW=((2, 576, D), BF),
    MIX=((2, D, D), BF),
    EI=((2, D, D), BF),
    EO=((2, D, D), BF),
    TT=((T, T), F32),
    TC=((T, T), F32),
    N1=((2, T, D), BF),
    QT=((2, 576, T), BF),
    PS=((2, 3, T, T), F32),
    OG=((2, D, T), BF),
    M=((2, T, D), F32),
    N2=((2, T, D), BF),
    PR=((2, T, NE), F32),
    GT=((2, T, 2), F32),
    HH=((2, 4, 256, 256), BF),
    XS=((2, 256, 1024), BF),
    XR=((2, 256, 1024), BF),
    YS=((2, 256, 1024), BF),
    YR=((2, 256, 1024), BF),
    DS=((2, 256, 1024), BF),
    DR=((2, 256, 1024), BF),
    ZS=((2, 256, 1024), BF),
    ZR=((2, 256, 1024), BF),
    XB=((2, 320, D), BF),
    AB=((2, 320, D), BF),
    GD=((2, 320, D), F32),
    DU=((320, D), BF),
    DY=((320, D), BF),
    PK=((2, 256, D), BF),
    US=((2, T, D), BF),
    UR=((2, NX, TR, D), BF),
    VS=((2, T, 896), BF),
    VR=((2, NX, TR, 896), BF),
    WS=((2, T, D), BF),
    WR=((2, NX, TR, D), BF),
    DM=((2, TR, D), F32),
    DMB=((2, T, D), BF),
    DQ=((2, 576, T), BF),
    GG=((T, D), BF),
    OUTB=((2, T, D), BF),
    EG=((2, 2, D, D), BF),
    EGR=((2, D, D), BF),
    G16=((2, D, D), BF),
    GP=((D, D), BF),
    GS=((D, D), BF),
    GR=((D, D), BF),
    SM=((2, 32, D), F32),
    SP=((32, D), F32),
    SU=((256, T), F32),
    SR=((256, T), F32),
    XU=((NX, 16, T), F32),
    SF=((256, T), F32),
)
NAMES = list(SCRATCH)


def body(ins, outs, V, SS, RS):
    bnd, seg, bkt, rts, slt, gns, qw_in, mx_in, tab, rt_in, ei_in, eo_in = ins
    bo, eg_own, eg_recv, gf, gains_o, router_o, bias_o = outs
    c = lax.axis_index("section")
    e = lax.axis_index("expert")
    r = lax.axis_index("head")
    mate = (1 - c, e, r)

    barrier = pltpu.get_barrier_semaphore()
    pl.semaphore_signal(barrier, inc=1, device_id=mate, device_id_type=MESH)
    for d in range(1, NX):
        pl.semaphore_signal(
            barrier, inc=1, device_id=(c, e, lax.rem(r + d, NX)), device_id_type=MESH
        )

    def greet(d, carry):
        pl.semaphore_signal(
            barrier, inc=1, device_id=(c, lax.rem(e + d, NE), r), device_id_type=MESH
        )
        return carry

    lax.fori_loop(1, NE, greet, 0)
    pl.semaphore_wait(barrier, 1 + (NX - 1) + (NE - 1))

    pending = []

    def wait_bytes(sem, ref):
        pltpu.make_async_copy(ref, ref, sem).wait()

    def remote(src, dst, name, device):
        k = sem_id(name)
        pltpu.make_async_remote_copy(
            src_ref=src,
            dst_ref=dst,
            send_sem=SS.at[k],
            recv_sem=RS.at[k],
            device_id=device,
            device_id_type=MESH,
        ).start()

    def recv(name, ref):
        wait_bytes(RS.at[sem_id(name)], ref)

    def later(name, ref):
        pending.append((name, ref))

    def share(name, own_src, mate_src, buf):
        k0 = sem_id(name + "0")
        assert sem_id(name + "1") == k0 + 1
        pltpu.make_async_remote_copy(
            src_ref=mate_src,
            dst_ref=buf.at[c],
            send_sem=SS.at[k0],
            recv_sem=RS.at[k0 + c],
            device_id=mate,
            device_id_type=MESH,
        ).start()
        pltpu.make_async_copy(own_src, buf.at[c], RS.at[k0 + c]).start()
        later(name + "0", buf.at[0])

    share("hb", bnd.at[c], bnd.at[1 - c], V["HB"])
    share("gn", gns, gns, V["GN"])
    share("qw", qw_in, qw_in, V["QW"])
    share("tb", tab, tab, V["TB"])
    pltpu.make_async_copy(seg, V["SEG"], RS.at[sem_id("seg")]).start()
    pltpu.make_async_copy(bkt, V["BK"], RS.at[sem_id("bk")]).start()
    share("ro", rts.at[c], rts.at[1 - c], V["RO"])
    share("sl", slt.at[c], slt.at[1 - c], V["SL"])

    def x_send(src, dst, name):
        for d in range(1, NX):
            peer = lax.rem(r + d, NX)
            remote(src(peer), dst, name, (c, e, peer))

    def mix_start(s):
        own = V["MIX"].at[s, pl.ds(pl.multiple_of(192 * r, 192), 192)]
        x_send(lambda peer: mx_in, own, "mix%d" % s)
        pltpu.make_async_copy(mx_in, own, RS.at[sem_id("mixo%d" % s)]).start()

    def mix_end(s):
        @pl.when(c == s)
        def _():
            recv("mix%d" % s, V["MIX"].at[s, pl.ds(0, 576)])
            wait_bytes(RS.at[sem_id("mixo%d" % s)], V["MIX"].at[s, pl.ds(0, 192)])
            remote(V["MIX"].at[s], V["MIX"].at[s], "mixr%d" % s, mate)
            wait_bytes(SS.at[sem_id("mix%d" % s)], V["MIX"].at[s, pl.ds(0, 576)])

        @pl.when(c != s)
        def _():
            recv("mixr%d" % s, V["MIX"].at[s])

    def mix_done(s):
        @pl.when(c == s)
        def _():
            wait_bytes(SS.at[sem_id("mixr%d" % s)], V["MIX"].at[s])

    @pl.when(c == 0)
    def _():
        mix_start(0)

    share("rt", rt_in, rt_in, V["RT"])
    share("ei", ei_in, ei_in, V["EI"])
    share("eo", eo_in, eo_in, V["EO"])

    def e_send(src, dst, rows, name):
        def step(d, carry):
            peer = lax.rem(e + d, NE)
            remote(
                src.at[pl.ds(pl.multiple_of(peer * rows, rows), rows)],
                dst.at[pl.ds(pl.multiple_of(e * rows, rows), rows)],
                name,
                (c, peer, r),
            )
            return carry

        lax.fori_loop(1, NE, step, 0)
        later(name, src.at[pl.ds(0, (NE - 1) * rows)])
        mine = pl.ds(pl.multiple_of(e * rows, rows), rows)
        dst[mine] = src[mine]

    def e_recv(dst, rows, name):
        recv(name, dst.at[pl.ds(0, (NE - 1) * rows)])

    recv("seg", V["SEG"])
    recv("bk", V["BK"])
    for s in range(2):
        recv("ro%d" % s, V["RO"].at[s])
        recv("sl%d" % s, V["SL"].at[s])
    V["TT"][...] = jnp.zeros((T, T), F32)
    V["TT"][0:1] = V["SEG"][c].astype(F32)
    V["TT"][8:10] = V["RO"][0].astype(F32)
    V["TT"][16:18] = V["RO"][1].astype(F32)
    V["TC"][...] = V["TT"][...].T
    allowed = (iota((T, T), 1) <= iota((T, T), 0)) & (V["TC"][:, 0:1] == V["TT"][0:1])
    hot = (iota((32, T), 0) == V["BK"][...]).astype(BF)
    flip = (((iota((T, T), 0) + iota((T, T), 1)) & (T - 1)) == 0).astype(BF)
    back_hot = nn(hot, flip).astype(BF)

    own_rows = pl.ds(pl.multiple_of(TR * r, TR), TR)

    def unit(x):
        scale = lax.rsqrt(jnp.mean(x * x, axis=-1, keepdims=True) + EPS)
        return x * scale, scale

    def attend(s, h_ref):
        hidden = h_ref[...].astype(F32)
        recv("gn%d" % s, V["GN"].at[s])
        n1 = (unit(hidden)[0] * V["GN"][s, 0:1]).astype(BF)
        V["N1"][s] = n1
        recv("qw%d" % s, V["QW"].at[s])
        V["QT"][s] = nt(V["QW"][s], n1).astype(BF)
        recv("tb%d" % s, V["TB"].at[s])
        table = V["TB"][s]
        high = table.astype(BF)
        mid = (table - high.astype(F32)).astype(BF)
        low = (table - high.astype(F32) - mid.astype(F32)).astype(BF)
        by_dist = nn(high, back_hot) + nn(mid, back_hot) + nn(low, back_hot)
        for h in range(3):
            bias = row_roll(jnp.broadcast_to(by_dist[h : h + 1], (T, T)), True)
            q = V["QT"][s, 64 * h : 64 * h + 64]
            k = V["QT"][s, 192 + 64 * h : 256 + 64 * h]
            v = V["QT"][s, 384 + 64 * h : 448 + 64 * h]
            score = jnp.where(allowed, tn(q, k) * SCALE + bias, NEG)
            top = jnp.max(score, axis=-1, keepdims=True)
            w = jnp.exp(score - top)
            w = w / jnp.sum(w, axis=-1, keepdims=True)
            V["PS"][s, h] = w
            V["OG"][s, pl.ds(pl.multiple_of(192 * r + 64 * h, 64), 64)] = nt(
                v, w.astype(BF)
            ).astype(BF)
        mine = V["OG"].at[s, pl.ds(pl.multiple_of(192 * r, 192), 192)]
        x_send(lambda peer: mine, mine, "og%d" % s)
        later("og%d" % s, V["OG"].at[s, pl.ds(0, 576)])
        route, slot = V["RO"][s], V["SL"][s]
        rows = iota((256, T), 0)
        for k in range(2):
            rk, sk = route[k : k + 1], slot[k : k + 1]
            lanes = slice(T * k, T * k + T)
            at = jnp.where(sk < 16, rk * 16 + sk, -1)
            V["HH"][s, 0, :, lanes] = (rows == at).astype(F32).astype(BF)
            extra = (sk >= 16) & (sk < CAP)
            for j in range(3):
                at = jnp.where(extra, rk * 16 + (4 * j - 16) + sk, -1)
                V["HH"][s, 1 + j, :, lanes] = (rows == at).astype(F32).astype(BF)
        mix_end(s)
        recv("og%d" % s, V["OG"].at[s, pl.ds(0, 576)])
        middle = hidden + tn(V["OG"][s], V["MIX"][s])
        V["M"][s] = middle
        n2 = (unit(middle)[0] * V["GN"][s, 1:2]).astype(BF)
        V["N2"][s] = n2

    def spread(s, pair, dst):
        dst[:, 0:D] = nn(V["HH"][s, 0], pair).astype(BF)
        extra = nn(V["HH"][s, 1], pair[:, 0:256])
        extra += nn(V["HH"][s, 2], pair[:, 256:512])
        extra += nn(V["HH"][s, 3], pair[:, 512:768])
        dst[:, D:1024] = extra.astype(BF)

    def gather(s, src):
        last = src[:, D:1024]
        return [
            tn(V["HH"][s, 0], src[:, 256 * j : 256 * j + 256]) + tn(V["HH"][s, 1 + j], last)
            for j in range(3)
        ]

    def gates(s):
        logits = nt(V["N2"][s], V["RT"][s])
        w = jnp.exp(logits - jnp.max(logits, axis=-1, keepdims=True))
        w = w / jnp.sum(w, axis=-1, keepdims=True)
        V["PR"][s] = w
        lane = iota((T, NE), 1).astype(F32)
        for k in range(2):
            col = V["TC"][:, 8 + 8 * s + k : 9 + 8 * s + k]
            V["GT"][s, :, k : k + 1] = jnp.sum(
                jnp.where(lane == col, w, 0.0), axis=-1, keepdims=True
            )

    def send_x(s):
        n2 = V["N2"][s]
        spread(s, jnp.concatenate([n2, n2], axis=0), V["XS"].at[s])
        e_send(V["XS"].at[s], V["XR"].at[s], 16, "x%d" % s)

    def send_dy(s, g_ref):
        g = g_ref[...].astype(F32)
        pair = [(V["GT"][s, :, k : k + 1] * g).astype(BF) for k in range(2)]
        spread(s, jnp.concatenate(pair, axis=0), V["DS"].at[s])
        e_send(V["DS"].at[s], V["DR"].at[s], 16, "d%d" % s)

    q_row, q_col = iota((64, 256), 0), iota((64, 256), 1)
    picks = [
        (q_col == (q_row // 4) * 16 + 4 * j + (q_row & 3)).astype(F32).astype(BF) for j in range(3)
    ]

    def unpack(src, dst):
        dst[0:256] = src[:, 0:D]
        for j in range(3):
            dst[256:320, 256 * j : 256 * j + 256] = nn(picks[j], src[:, D:1024]).astype(BF)

    def pack(value, dst):
        dst[:, 0:D] = value[0:256].astype(BF)
        extra = tn(picks[0], value[256:320, 0:256].astype(BF))
        extra += tn(picks[1], value[256:320, 256:512].astype(BF))
        extra += tn(picks[2], value[256:320, 512:768].astype(BF))
        dst[:, D:1024] = extra.astype(BF)

    def expert_forward(s):
        e_recv(V["XR"].at[s], 16, "x%d" % s)
        unpack(V["XR"].at[s], V["XB"].at[s])
        v = nn(V["XB"][s], V["EI"][s])
        v2 = v * v
        th = jnp.tanh(0.7978845608028654 * (v + 0.044715 * v * v2))
        V["AB"][s] = (0.5 * v * (1.0 + th)).astype(BF)
        V["GD"][s] = 0.5 * (1.0 + th) + 0.5 * v * (1.0 - th * th) * (
            0.7978845608028654 * (1.0 + 3.0 * 0.044715 * v2)
        )
        pack(nn(V["AB"][s], V["EO"][s]), V["YS"].at[s])
        e_send(V["YS"].at[s], V["YR"].at[s], 16, "y%d" % s)

    def expert_backward(s):
        e_recv(V["DR"].at[s], 16, "d%d" % s)
        unpack(V["DR"].at[s], V["DY"])
        V["DU"][...] = (nt(V["DY"][...], V["EO"][s]) * V["GD"][s]).astype(BF)
        pack(nt(V["DU"][...], V["EI"][s]), V["ZS"].at[s])
        e_send(V["ZS"].at[s], V["ZR"].at[s], 16, "z%d" % s)
        V["EG"][s, 1] = tn(V["AB"][s], V["DY"][...]).astype(BF)
        V["EG"][s, 0] = tn(V["XB"][s], V["DU"][...]).astype(BF)

        @pl.when(c != s)
        def _():
            remote(V["EG"].at[s], V["EGR"], "eg", mate)

    def tok_send(buf, dst, s, name):
        x_send(
            lambda peer: buf.at[s, pl.ds(pl.multiple_of(TR * peer, TR), TR)],
            dst.at[s, r],
            name + str(s),
        )
        later(name + str(s), buf.at[s, pl.ds(0, 3 * TR)])
        dst[s, r] = buf[s, own_rows]

    def tok_recv(dst, s, name):
        recv(name + str(s), dst.at[s, pl.ds(0, 3)])
        total = dst[s, 0].astype(F32)
        for k in range(1, NX):
            total += dst[s, k].astype(F32)
        return total

    def tok_share(value, ref, name):
        ref[own_rows] = value
        mine = ref.at[own_rows]
        x_send(lambda peer: mine, mine, name)
        later(name, ref.at[pl.ds(0, 3 * TR)])

    def combine(s):
        e_recv(V["YR"].at[s], 16, "y%d" % s)
        parts = gather(s, V["YR"].at[s])
        g0, g1 = V["GT"][s, :, 0:1], V["GT"][s, :, 1:2]
        for j in range(3):
            lanes = slice(256 * j, 256 * j + 256)
            V["PK"][s, :, lanes] = parts[j].astype(BF)
            V["US"][s, :, lanes] = (g0 * parts[j][0:T] + g1 * parts[j][T:]).astype(BF)

    def send_out(s):
        tok_send(V["US"], V["UR"], s, "u")

    def finish_out(s, ref):
        out = V["M"][s, own_rows] + tok_recv(V["UR"], s, "u")
        tok_share(out.astype(BF), ref, "h%d" % s)

    def token_grads(s, g_ref):
        g = g_ref[...].astype(F32)
        lane = iota((T, T), 1)
        picked = V["PK"][s]
        d0 = jnp.sum(g * picked[0:T].astype(F32), axis=-1, keepdims=True)
        d1 = jnp.sum(g * picked[T:].astype(F32), axis=-1, keepdims=True)
        V["VS"][s, :, D:896] = jnp.where(lane == 0, d0, jnp.where(lane == 1, d1, 0.0)).astype(BF)
        e_recv(V["ZR"].at[s], 16, "z%d" % s)
        parts = gather(s, V["ZR"].at[s])
        for j in range(3):
            V["VS"][s, :, 256 * j : 256 * j + 256] = (parts[j][0:T] + parts[j][T:]).astype(BF)
        tok_send(V["VS"], V["VR"], s, "v")

    def middle_grads(s, g_ref):
        total = tok_recv(V["VR"], s, "v")
        gain = V["GN"][s, 1:2]
        u2, r2 = unit(V["M"][s, own_rows])
        pr = V["PR"][s, own_rows]
        lane = iota((TR, NE), 1).astype(F32)
        cols = V["TC"][own_rows]
        dpr = jnp.where(lane == cols[:, 8 + 8 * s : 9 + 8 * s], total[:, D : D + 1], 0.0)
        dpr += jnp.where(lane == cols[:, 9 + 8 * s : 10 + 8 * s], total[:, D + 1 : D + 2], 0.0)
        dl = (pr * (dpr - jnp.sum(pr * dpr, axis=-1, keepdims=True))).astype(BF)
        dn2 = total[:, 0:D] + nn(dl, V["RT"][s])
        du = dn2 * gain
        dm = g_ref[own_rows].astype(F32) + r2 * (
            du - u2 * jnp.mean(du * u2, axis=-1, keepdims=True)
        )
        V["DM"][s] = dm
        tok_share(dm.astype(BF), V["DMB"].at[s], "m%d" % s)
        V["SM"][s, 0:16] = tn(dl, V["N2"][s, own_rows])
        V["SM"][s, 16:32] = jnp.zeros((16, D), F32)
        V["SM"][s, 17:18] = jnp.sum(dn2 * u2, axis=0, keepdims=True)

    def attend_backward(s, h_ref):
        u1, _ = unit(h_ref[...].astype(F32))
        recv("m%d" % s, V["DMB"].at[s, pl.ds(0, 3 * TR)])
        dmb = V["DMB"][s]
        do = nt(V["MIX"][s, pl.ds(pl.multiple_of(192 * r, 192), 192)], dmb).astype(BF)
        sums = []
        for h in range(3):
            q = V["QT"][s, 64 * h : 64 * h + 64]
            k = V["QT"][s, 192 + 64 * h : 256 + 64 * h]
            v = V["QT"][s, 384 + 64 * h : 448 + 64 * h]
            doh = do[64 * h : 64 * h + 64]
            w = V["PS"][s, h]
            dw = tn(doh, v)
            dsc = w * (dw - jnp.sum(w * dw, axis=-1, keepdims=True))
            low = dsc.astype(BF)
            V["DQ"][s, 64 * h : 64 * h + 64] = (nt(k, low) * SCALE).astype(BF)
            V["DQ"][s, 192 + 64 * h : 256 + 64 * h] = (nn(q, low) * SCALE).astype(BF)
            V["DQ"][s, 384 + 64 * h : 448 + 64 * h] = nn(doh, w.astype(BF)).astype(BF)
            sums.append(dsc)
        dn1 = tn(V["DQ"][s], V["QW"][s])
        V["WS"][s] = dn1.astype(BF)
        tok_send(V["WS"], V["WR"], s, "w")
        V["SM"][s, 16:17] = jnp.sum(dn1 * u1, axis=0, keepdims=True)
        for h in range(3):
            turned = jnp.sum(row_roll(sums[h], False), axis=0, keepdims=True)
            turned = jnp.sum(
                jnp.broadcast_to(turned, (32, T)) * back_hot.astype(F32), axis=-1, keepdims=True
            )
            spot = (iota((32, T), 0) == iota((32, T), 1)).astype(F32)
            V["SM"][s, 18 + h : 19 + h, 0:T] = jnp.sum(turned * spot, axis=0, keepdims=True)
        V["G16"][s, 0:576] = nn(V["DQ"][s], V["N1"][s]).astype(BF)
        V["G16"][s, 576:768] = nn(
            V["OG"][s, pl.ds(pl.multiple_of(192 * r, 192), 192)], dmb
        ).astype(BF)

        @pl.when(c != s)
        def _():
            remote(V["G16"].at[s], V["GP"], "gp", mate)
            remote(V["SM"].at[s], V["SP"], "sp", mate)

    def finish_hidden(s, h_ref, ref):
        dn1 = tok_recv(V["WR"], s, "w")
        u1, r1 = unit(h_ref[own_rows].astype(F32))
        du = dn1 * V["GN"][s, 0:1]
        dh = V["DM"][s] + r1 * (du - u1 * jnp.mean(du * u1, axis=-1, keepdims=True))
        tok_share(dh.astype(BF), ref, "g%d" % s)

    h0, g1 = V["HB"].at[0], V["HB"].at[1]
    recv("hb0", h0)
    attend(0, h0)
    recv("rt0", V["RT"].at[0])

    @pl.when(c == 1)
    def _():
        mix_start(1)

    send_x(0)
    gates(0)
    recv("ei0", V["EI"].at[0])
    recv("eo0", V["EO"].at[0])
    expert_forward(0)
    combine(0)
    send_out(0)
    finish_out(0, V["HX"])
    recv("h0", V["HX"].at[pl.ds(0, 3 * TR)])

    attend(1, V["HX"])
    send_x(1)
    recv("rt1", V["RT"].at[1])
    gates(1)
    recv("hb1", g1)
    send_dy(1, g1)
    recv("ei1", V["EI"].at[1])
    recv("eo1", V["EO"].at[1])
    expert_forward(1)
    expert_backward(1)
    combine(1)
    token_grads(1, g1)
    send_out(1)
    middle_grads(1, g1)
    finish_out(1, V["OUTB"].at[1])
    attend_backward(1, V["HX"])
    finish_hidden(1, V["HX"], V["GG"])
    recv("g1", V["GG"].at[pl.ds(0, 3 * TR)])

    send_dy(0, V["GG"])
    expert_backward(0)
    token_grads(0, V["GG"])
    middle_grads(0, V["GG"])
    attend_backward(0, h0)
    finish_hidden(0, h0, V["OUTB"].at[0])

    recv("gp", V["GP"])
    V["GS"][...] = (V["G16"][c].astype(F32) + V["GP"][...].astype(F32)).astype(BF)
    e_send(V["GS"], V["GR"], 48, "gr")
    recv("sp", V["SP"])
    small = V["SM"][c] + V["SP"][...]
    V["SU"][...] = jnp.zeros((256, T), F32)
    for j in range(12):
        V["SU"][16 * j : 16 * j + 16] = small[
            16 * (j // 6) : 16 * (j // 6) + 16, T * (j % 6) : T * (j % 6) + T
        ]
    e_send(V["SU"], V["SR"], 16, "sr")
    recv("g0", V["OUTB"].at[0, pl.ds(0, 3 * TR)])
    recv("h1", V["OUTB"].at[1, pl.ds(0, 3 * TR)])
    remote(V["OUTB"].at[1 - c], bo.at[c], "bo", mate)
    later("bo", V["OUTB"].at[0])
    pltpu.make_async_copy(V["OUTB"].at[c], bo.at[c], RS.at[sem_id("boo")]).start()
    pltpu.make_async_copy(V["EG"].at[c], eg_own, RS.at[sem_id("ego")]).start()
    recv("eg", V["EGR"])
    pltpu.make_async_copy(V["EGR"], eg_recv, RS.at[sem_id("egc")]).start()

    e_recv(V["SR"], 16, "sr")
    tiny = V["SR"][0:16]
    for j in range(1, NE):
        tiny += V["SR"][16 * j : 16 * j + 16]
    V["XU"][r] = tiny
    x_send(lambda peer: V["XU"].at[r], V["XU"].at[r], "xu")
    later("xu", V["XU"].at[pl.ds(0, 3)])
    e_recv(V["GR"], 48, "gr")
    total = V["GR"][0:48].astype(F32)
    for j in range(1, NE):
        total += V["GR"][48 * j : 48 * j + 48].astype(F32)
    gather_rows = pl.ds(pl.multiple_of(48 * e, 48), 48)
    gf[gather_rows] = total.astype(BF)

    def e_share(ref, rows, name):
        mine = ref.at[rows]

        def step(d, carry):
            remote(mine, mine, name, (c, lax.rem(e + d, NE), r))
            return carry

        lax.fori_loop(1, NE, step, 0)

    e_share(gf, gather_rows, "gf")
    later("gf", gf.at[pl.ds(0, 15 * 48)])
    recv("xu", V["XU"].at[pl.ds(0, 3)])
    summed = V["XU"][0] + V["XU"][1] + V["XU"][2] + V["XU"][3]
    line = iota((16, T), 0)
    held = (e >= 6) & (line >= 2) & (line <= 4)
    unit_rows = pl.ds(pl.multiple_of(16 * e, 16), 16)
    V["SF"][unit_rows] = jnp.where(held, V["XU"][r], summed)
    e_share(V["SF"], unit_rows, "sf")
    later("sf", V["SF"].at[pl.ds(0, 240)])
    recv("sf", V["SF"].at[pl.ds(0, 240)])
    for j in range(6):
        lanes = slice(T * j, T * j + T)
        router_o[:, lanes] = V["SF"][16 * j : 16 * j + 16]
        gains_o[:, lanes] = V["SF"][96 + 16 * j : 98 + 16 * j]
    bias_o[...] = V["SF"][98:101]
    recv("gf", gf.at[pl.ds(0, 15 * 48)])
    recv("bo", bo.at[0])
    recv("boo", bo.at[0])
    recv("ego", eg_own)
    recv("egc", eg_recv)
    for name, ref in pending:
        wait_bytes(SS.at[sem_id(name)], ref)
    wait_bytes(SS.at[sem_id("eg")], V["EGR"])
    wait_bytes(SS.at[sem_id("gp")], V["GP"])
    wait_bytes(SS.at[sem_id("sp")], V["SP"])
    for s in range(2):
        mix_done(s)


def kernel(*refs):
    ins, outs = refs[:12], refs[12:19]
    V = dict(zip(NAMES, refs[19:]))
    SS, RS = refs[-2:]
    body(ins, outs, V, SS, RS)


N_SEMS = 80


def on_device(
    boundary,
    segments,
    buckets,
    routes,
    slots,
    gains,
    qkv_weight,
    mix_weight,
    bias_table,
    router,
    expert_in,
    expert_out,
):
    qkv = jnp.transpose(qkv_weight[0], (1, 2, 0)).reshape(576, D)
    any_space = pl.BlockSpec(memory_space=pl.ANY)
    vmem = pl.BlockSpec(memory_space=pltpu.VMEM)
    shape = jax.ShapeDtypeStruct
    outs = pl.pallas_call(
        kernel,
        out_shape=[
            shape((2, T, D), BF),
            shape((2, D, D), BF),
            shape((2, D, D), BF),
            shape((D, D), BF),
            shape((2, D), F32),
            shape((NE, D), F32),
            shape((3, T), F32),
        ],
        in_specs=[any_space] * 12,
        out_specs=[vmem, any_space, any_space, vmem, vmem, vmem, vmem],
        scratch_shapes=[pltpu.VMEM(*SCRATCH[name]) for name in NAMES]
        + [pltpu.SemaphoreType.DMA((N_SEMS,)), pltpu.SemaphoreType.DMA((N_SEMS,))],
        compiler_params=pltpu.CompilerParams(
            collective_id=0, has_side_effects=True, vmem_limit_bytes=60 * 1024 * 1024
        ),
    )(
        boundary[0],
        segments,
        buckets.reshape(1, T),
        jnp.transpose(routes[0], (0, 2, 1)),
        jnp.transpose(slots[0], (0, 2, 1)),
        gains[0],
        qkv,
        mix_weight[0],
        jnp.transpose(bias_table[0]),
        jnp.transpose(router[0]),
        expert_in[0, 0],
        expert_out[0, 0],
    )
    bo, eg_own, eg_recv, gf, grad_gains, grad_router, grad_bias = outs
    grad_expert = eg_own.astype(F32) + eg_recv.astype(F32)
    grad_qkv = jnp.transpose(gf[:576].astype(F32).reshape(3, 192, D), (2, 0, 1))
    return (
        bo[None],
        grad_gains[None],
        grad_qkv[None],
        gf[576:].astype(F32)[None],
        jnp.transpose(grad_bias[:, :32])[None],
        jnp.transpose(grad_router)[None],
        grad_expert[0][None, None],
        grad_expert[1][None, None],
    )


def solution(mesh):
    in_specs = (
        P("section", None, "expert", None),
        P(None, "expert", None),
        P(),
        P("section", None, "expert", None),
        P("section", None, "expert", None),
        P("section", None, None),
        P("section", None, None, "head"),
        P("section", "head", None),
        P("section", None, "head"),
        P("section", None, None),
        P("section", "expert", None, "head"),
        P("section", "expert", "head", None),
    )
    out_specs = (
        P("section", None, "expert", None),
        P("section", None, None),
        P("section", None, None, "head"),
        P("section", "head", None),
        P("section", None, "head"),
        P("section", None, None),
        P("section", "expert", None, "head"),
        P("section", "expert", "head", None),
    )
    return jax.shard_map(
        on_device, mesh=mesh, in_specs=in_specs, out_specs=out_specs, check_vma=False
    )
```

time: 962 us -> 191 us (0.20); the launches traced: 949 us -> 191 us
  waiting for transfers between devices: 285 us -> 0 us
  blocking collectives: 262 us -> 0 us
  Pallas kernels: 0 us -> 179 us
  local copies, waits for them, and re-layouts: 184 us -> 6.35 us
  matrix products: 98.1 us -> 0 us
  starting transfers between devices: 57.5 us -> 0 us
  other arithmetic: 46.1 us -> 5.09 us
  between operations: 16.6 us -> 0.68 us
    psum x6 -> x0, blocking collectives: 226 us -> none  [the longest x5 151 us: to_source(): summed = lax.psum(partial_value, 'head').astype(jnp.bfloat16)]
    psum x7 -> x0, waiting for transfers between devices: 224 us -> none  [the longest x6 206 us: mixer_total(): return lax.psum(partial_value, 'head')]
    pallas_call x0 -> x1, Pallas kernels: none -> 179 us  [on_device(): pl.pallas_call(kernel, out_shape=[shape((2, T, D), BF), shape((2, D, D),...]
    gather x2 -> x0, local copies, waits for them, and re-layouts: 97.3 us -> none  [on_device(): pair_bucket = buckets[distance]]
    dot_general x73 -> x0, matrix products: 91 us -> none  [the longest x12 23.5 us: contract_rows(): lax.dot_general(left, right, (((0,), (0,)), ((), ())), precision=precise,...]
    all_to_all x10 -> x0, waiting for transfers between devices: 59.7 us -> none  [the longest x6 36.3 us: to_source(): lax.all_to_all(summed.reshape(sources, capacity, -1), 'expert', split_axi...]
    all_to_all x10 -> x0, starting transfers between devices: 51.6 us -> none  [the longest x6 26.1 us: to_source(): lax.all_to_all(summed.reshape(sources, capacity, -1), 'expert', split_axi...]
    reshape x24 -> x0, local copies, waits for them, and re-layouts: 46.1 us -> none  [the longest x6 11.7 us: to_source(): summed.reshape(sources, capacity, -1)]
  transfers between devices with their start and end apart: 21 -> 0, of which waited for: 19 -> 0; matrix products, arithmetic and copies ran while one was open for 9% -> 0% of each run, Pallas kernels for 0% -> 0%
where the time goes in v1:
time: 191 us
  Pallas kernels  179 us (94%)
  local copies, waits for them, and re-layouts  6.35 us (3%)
  other arithmetic  5.09 us (3%)
    pallas_call x1, Pallas kernels, on_device(): pl.pallas_call(kernel, out_shape=[shape((2, T, D), BF), shape((2, D, D),...  179 us

profile of v1, /device:TPU:0, one launch (start us, length us, event | category | flops | bytes accessed | tf_op | source)
XLA Modules:
  0.0 190.7 jit_solution(12601882648939662998)
XLA Ops:
  0.6 1.3 copy.23
  1.9 178.5 %shard_map.179 = (bf16[2,128,768]{2,1,0:T(8,128)(2,1)}, bf16[2,768,768]{2,1,0:T(8,128)(2,1)}, bf16[2,768,768]{2,1,0:T(8,128)(2,1)}, bf16[768,768]{1,0:T(8,128)(2...) custom-call(bf16[2,128,768]{2,1,0:T(8,128)(2,1)} %bitcast.52, s32[2,1,128]{2,1,0:T(1,128)} %refs_1_.1, ...), custom_call_target="tpu_custom_call" | custom-call | tf_op jit(solution)/shard_map/pallas_call | solution.py:656
  180.4 2.9 %convert_add_fusion = f32[2,768,768]{2,1,0:T(8,128)S(1)} fusion(bf16[2,768,768]{2,1,0:T(8,128)(2,1)} %get-tuple-element.21, bf16[2,768,768]{2,1,0:T(8,128)(2,1)} %get-tuple-element.20), kind=kLoop, calls=%fused_computation | loop fusion | flops 3538944 | bytes 9437184 | tf_op jit(solution)/shard_map/add | solution.py:689
  183.3 0.0 copy-start
  183.3 2.5 %slice_bitcast_fusion = (f32[1,1,768,768]{3,2,1,0:T(8,128)}, f32[1,1,768,768]{3,2,1,0:T(8,128)}) fusion(f32[2,768,768]{2,1,0:T(8,128)S(1)} %convert_add_fusion), kind=kLoop, calls=%fused_computation.1 | loop fusion | bytes 9437184 | tf_op jit(solution)/shard_map/broadcast_in_dim;squeeze | solution.py:699
  185.8 0.0 copy-done
  185.8 0.0 copy-start.4
  185.8 0.0 copy-start.1
  185.8 0.1 slice.15
  185.9 0.0 copy-start.3
  185.9 0.0 copy-start.2
  185.9 1.4 convert_bitcast_fusion
  187.3 0.9 bitcast_convert_fusion
  188.1 0.0 copy-done.4
  188.1 0.6 copy.20
  188.7 0.0 copy-done.1
  188.7 0.7 copy.27
  189.4 0.0 copy-done.3
  189.5 0.6 copy.28
  190.0 0.0 copy-done.2
  190.0 0.6 copy.29
  (1 shorter events, 0.0 us)
Async XLA Ops:
  183.3 2.5 %copy-start = (bf16[768,768]{1,0:T(8,128)(2,1)S(1)}, bf16[768,768]{1,0:T(8,128)(2,1)}, u32[]{:S(2)}) copy-start(bf16[768,768]{1,0:T(8,128)(2,1)} %get-tuple-element.17) | copy-start | bytes 3538948
  185.8 2.3 %copy-start.4 = (f32[3,128]{1,0:T(4,128)S(1)}, f32[3,128]{1,0:T(4,128)}, u32[]{:S(2)}) copy-start(f32[3,128]{1,0:T(4,128)} %get-tuple-element.18) | copy-start | bytes 4612
  185.8 2.9 %copy-start.1 = (bf16[2,128,768]{2,1,0:T(8,128)(2,1)S(1)}, bf16[2,128,768]{2,1,0:T(8,128)(2,1)}, u32[]{:S(2)}) copy-start(bf16[2,128,768]{2,1,0:T(8,128)(2,1)} %get-tuple-element.15) | copy-start | bytes 1179652
  185.9 3.5 %copy-start.3 = (f32[2,768]{1,0:T(2,128)S(1)}, f32[2,768]{1,0:T(2,128)}, u32[]{:S(2)}) copy-start(f32[2,768]{1,0:T(2,128)} %get-tuple-element.16) | copy-start | bytes 18436
  185.9 4.1 %copy-start.2 = (f32[16,768]{1,0:T(8,128)S(1)}, f32[16,768]{1,0:T(8,128)}, u32[]{:S(2)}) copy-start(f32[16,768]{1,0:T(8,128)} %get-tuple-element.19) | copy-start | bytes 147460

commit v2 on v1

v2 whole, which is shorter than its diff:
```python
import types

import jax
import jax.numpy as jnp
from jax import lax
from jax.experimental import pallas as pl
from jax.experimental.pallas import tpu as pltpu
from jax.sharding import PartitionSpec as P

MESH = pl.DeviceIdType.MESH
EPS = 1e-06
NEG = -1e30
BF = jnp.bfloat16
F32 = jnp.float32
T = 128
D = 768
NE = 16
NX = 4
CAP = 20
TR = T // NX
SCALE = 0.125


def nn(a, b):
    return lax.dot_general(a, b, (((1,), (0,)), ((), ())), preferred_element_type=F32)


def nt(a, b):
    return lax.dot_general(a, b, (((1,), (1,)), ((), ())), preferred_element_type=F32)


def tn(a, b):
    return lax.dot_general(a, b, (((0,), (0,)), ((), ())), preferred_element_type=F32)


def iota(shape, dim):
    return lax.broadcasted_iota(jnp.int32, shape, dim)


def row_roll(x, right):
    rows = iota((T, T), 0)
    for bit in range(7):
        step = 1 << bit
        turned = pltpu.roll(x, step if right else T - step, 1)
        x = jnp.where((rows >> bit) & 1 == 1, turned, x)
    return x


ORDER = [(0, 0), (0, 1), (0, 3), (1, 0), (3, 0), (1, 1), (3, 3), (1, 3)]
ORDER += [(3, 1), (0, 2), (2, 0), (1, 2), (3, 2), (2, 1), (2, 3), (2, 2)]
HALF = 160

SEMS = {}


def sem_id(name):
    return SEMS.setdefault(name, len(SEMS))


SCRATCH = dict(
    HB=((2, T, D), BF),
    HX=((T, D), BF),
    SEG=((2, 1, T), jnp.int32),
    BK=((1, T), jnp.int32),
    RO=((2, 2, T), jnp.int32),
    SL=((2, 2, T), jnp.int32),
    GN=((2, 2, D), F32),
    TB=((2, 3, 1, 32), F32),
    RT=((2, NE, D), BF),
    QW=((2, 576, D), BF),
    MIX=((2, D, D), BF),
    EI=((2, D, D), BF),
    EO=((2, D, D), BF),
    TT=((T, T), F32),
    TC=((T, T), F32),
    N1=((2, T, D), BF),
    QT=((2, 576, T), BF),
    PS=((2, 3, T, T), F32),
    OG=((2, D, T), BF),
    M=((2, T, D), F32),
    N2=((2, T, D), BF),
    PR=((2, T, NE), F32),
    GT=((2, T, 2), F32),
    HH=((2, 4, 256, 256), BF),
    XS=((2, 256, 1024), BF),
    XR=((2, 256, 1024), BF),
    YS=((2, 256, 1024), BF),
    YR=((2, 256, 1024), BF),
    DS=((2, 256, 1024), BF),
    DR=((2, 256, 1024), BF),
    ZS=((2, 256, 1024), BF),
    ZR=((2, 256, 1024), BF),
    XB=((2, 320, D), BF),
    AB=((2, 320, D), BF),
    GD=((2, 320, D), F32),
    DU=((320, D), BF),
    DY=((320, D), BF),
    PK=((2, 256, D), BF),
    US=((2, T, D), BF),
    UR=((2, NX, TR, D), BF),
    VS=((2, T, 896), BF),
    VR=((2, NX, TR, 896), BF),
    WS=((2, T, D), BF),
    WR=((2, NX, TR, D), BF),
    QS=((2, NX * 208, T), BF),
    QR=((2, NX, 208, T), BF),
    R2=((2, 1, T), F32),
    GM=((192, T), F32),
    UM=((192, T), F32),
    DM=((2, TR, D), F32),
    DMB=((2, T, D), BF),
    DQ=((2, 576, T), BF),
    SC=((3, T, T), F32),
    GG=((T, D), BF),
    OUTB=((2, T, D), BF),
    EG=((2, 2, D, D), BF),
    EGR=((2, D, D), BF),
    G16=((2, D, D), BF),
    GP=((D, D), BF),
    GS=((D, D), BF),
    GR=((D, D), BF),
    SM=((2, 32, D), F32),
    SP=((32, D), F32),
    SU=((256, T), F32),
    SR=((256, T), F32),
    XU=((NX, 16, T), F32),
    SF=((256, T), F32),
)
NAMES = list(SCRATCH)


def body(ins, outs, V, SS, RS):
    bnd, seg, bkt, rts, slt, gns, qw_in, mx_in, tab, rt_in, ei_in, eo_in = ins
    bo, eg_own, eg_recv, gf, gains_o, router_o, bias_o = outs
    c = lax.axis_index("section")
    e = lax.axis_index("expert")
    r = lax.axis_index("head")
    mate = (1 - c, e, r)

    barrier = pltpu.get_barrier_semaphore()
    pl.semaphore_signal(barrier, inc=1, device_id=mate, device_id_type=MESH)
    for d in range(1, NX):
        pl.semaphore_signal(
            barrier, inc=1, device_id=(c, e, lax.rem(r + d, NX)), device_id_type=MESH
        )

    def greet(d, carry):
        pl.semaphore_signal(
            barrier, inc=1, device_id=(c, lax.rem(e + d, NE), r), device_id_type=MESH
        )
        return carry

    lax.fori_loop(1, NE, greet, 0)
    pl.semaphore_wait(barrier, 1 + (NX - 1) + (NE - 1))

    pending = []

    def wait_bytes(sem, ref):
        pltpu.make_async_copy(ref, ref, sem).wait()

    def remote(src, dst, name, device):
        k = sem_id(name)
        pltpu.make_async_remote_copy(
            src_ref=src,
            dst_ref=dst,
            send_sem=SS.at[k],
            recv_sem=RS.at[k],
            device_id=device,
            device_id_type=MESH,
        ).start()

    def recv(name, ref):
        wait_bytes(RS.at[sem_id(name)], ref)

    def later(name, ref):
        pending.append((name, ref))

    def share(name, own_src, mate_src, buf):
        k0 = sem_id(name + "0")
        assert sem_id(name + "1") == k0 + 1
        pltpu.make_async_remote_copy(
            src_ref=mate_src,
            dst_ref=buf.at[c],
            send_sem=SS.at[k0],
            recv_sem=RS.at[k0 + c],
            device_id=mate,
            device_id_type=MESH,
        ).start()
        pltpu.make_async_copy(own_src, buf.at[c], RS.at[k0 + c]).start()
        later(name + "0", buf.at[0])

    share("hb", bnd.at[c], bnd.at[1 - c], V.HB)
    share("gn", gns, gns, V.GN)
    share("qw", qw_in, qw_in, V.QW)
    share("tb", tab, tab, V.TB)
    pltpu.make_async_copy(seg, V.SEG, RS.at[sem_id("seg")]).start()
    pltpu.make_async_copy(bkt, V.BK, RS.at[sem_id("bk")]).start()
    share("ro", rts.at[c], rts.at[1 - c], V.RO)
    share("sl", slt.at[c], slt.at[1 - c], V.SL)

    def x_send(src, dst, name):
        for d in range(1, NX):
            peer = lax.rem(r + d, NX)
            remote(src(peer), dst, name, (c, e, peer))

    def mix_start(s):
        own = V.MIX.at[s, pl.ds(pl.multiple_of(192 * r, 192), 192)]
        x_send(lambda peer: mx_in, own, "mix%d" % s)
        pltpu.make_async_copy(mx_in, own, RS.at[sem_id("mixo%d" % s)]).start()

    def mix_end(s):
        @pl.when(c == s)
        def _():
            recv("mix%d" % s, V.MIX.at[s, pl.ds(0, 576)])
            wait_bytes(RS.at[sem_id("mixo%d" % s)], V.MIX.at[s, pl.ds(0, 192)])
            remote(V.MIX.at[s], V.MIX.at[s], "mixr%d" % s, mate)
            wait_bytes(SS.at[sem_id("mix%d" % s)], V.MIX.at[s, pl.ds(0, 576)])

        @pl.when(c != s)
        def _():
            recv("mixr%d" % s, V.MIX.at[s])

    def mix_done(s):
        @pl.when(c == s)
        def _():
            wait_bytes(SS.at[sem_id("mixr%d" % s)], V.MIX.at[s])

    @pl.when(c == 0)
    def _():
        mix_start(0)

    share("rt", rt_in, rt_in, V.RT)
    share("ei", ei_in, ei_in, V.EI)
    share("eo", eo_in, eo_in, V.EO)

    def e_send(src, dst, rows, name, note=True):
        def step(d, carry):
            peer = lax.rem(e + d, NE)
            remote(
                src.at[pl.ds(pl.multiple_of(peer * rows, rows), rows)],
                dst.at[pl.ds(pl.multiple_of(e * rows, rows), rows)],
                name,
                (c, peer, r),
            )
            return carry

        lax.fori_loop(1, NE, step, 0)
        if note:
            later(name, src.at[pl.ds(0, (NE - 1) * rows)])
        mine = pl.ds(pl.multiple_of(e * rows, rows), rows)
        dst[mine] = src[mine]

    def e_recv(dst, rows, name):
        recv(name, dst.at[pl.ds(0, (NE - 1) * rows)])

    def e_out(src, dst, name):
        dst[0:16] = src[pl.ds(pl.multiple_of(16 * e, 16), 16)]
        for p, (dy, dz) in enumerate(ORDER[1:], 1):
            peer = lax.rem(e // 4 + dy, 4) * 4 + lax.rem(lax.rem(e, 4) + dz, 4)
            remote(
                src.at[pl.ds(pl.multiple_of(16 * peer, 16), 16)],
                dst.at[pl.ds(16 * p, 16)],
                name + "ab"[p // 8],
                (c, peer, r),
            )
        later(name + "a", src.at[pl.ds(0, 112)])
        later(name + "b", src.at[pl.ds(0, 128)])

    def e_half(dst, name, g):
        recv(name + "ab"[g], dst.at[pl.ds(0, 112 + 16 * g)])

    def e_back(src, dst, name, g):
        if g == 0:
            dst[pl.ds(pl.multiple_of(16 * e, 16), 16)] = src[0:16]
        else:
            later(name, src.at[pl.ds(0, 240)])
        for p in range(max(1, 8 * g), 8 * g + 8):
            dy, dz = ORDER[p]
            peer = lax.rem(e // 4 + 4 - dy, 4) * 4 + lax.rem(lax.rem(e, 4) + 4 - dz, 4)
            remote(
                src.at[pl.ds(16 * p, 16)],
                dst.at[pl.ds(pl.multiple_of(16 * e, 16), 16)],
                name,
                (c, peer, r),
            )

    recv("seg", V.SEG)
    recv("bk", V.BK)
    for s in range(2):
        recv("ro%d" % s, V.RO.at[s])
        recv("sl%d" % s, V.SL.at[s])
    V.TT[...] = jnp.zeros((T, T), F32)
    V.TT[0:1] = V.SEG[c].astype(F32)
    V.TT[8:10] = V.RO[0].astype(F32)
    V.TT[16:18] = V.RO[1].astype(F32)
    V.TT[24:26] = V.SL[0].astype(F32)
    V.TT[32:34] = V.SL[1].astype(F32)
    V.TC[...] = V.TT[...].T
    allowed = (iota((T, T), 1) <= iota((T, T), 0)) & (V.TC[:, 0:1] == V.TT[0:1])
    hot = (iota((32, T), 0) == V.BK[...]).astype(BF)
    flip = (((iota((T, T), 0) + iota((T, T), 1)) & (T - 1)) == 0).astype(BF)
    back_hot = nn(hot, flip).astype(BF)

    own_rows = pl.ds(pl.multiple_of(TR * r, TR), TR)

    def unit(x):
        scale = lax.rsqrt(jnp.mean(x * x, axis=-1, keepdims=True) + EPS)
        return x * scale, scale

    def row_sums(x):
        ones = jnp.ones((16, D), BF)
        high = x.astype(BF)
        return nt(ones, high) + nt(ones, (x - high.astype(F32)).astype(BF))

    def one_hots(s):
        route, slot = V.RO[s], V.SL[s]
        rows = iota((256, T), 0)
        for k in range(2):
            rk, sk = route[k : k + 1], slot[k : k + 1]
            lanes = slice(T * k, T * k + T)
            at = jnp.where(sk < 16, rk * 16 + sk, -1)
            V.HH[s, 0, :, lanes] = (rows == at).astype(F32).astype(BF)
            extra = (sk >= 16) & (sk < CAP)
            for j in range(3):
                at = jnp.where(extra, rk * 16 + (4 * j - 16) + sk, -1)
                V.HH[s, 1 + j, :, lanes] = (rows == at).astype(F32).astype(BF)

    def attend(s, h_ref):
        hidden = h_ref[...].astype(F32)
        recv("gn%d" % s, V.GN.at[s])
        n1 = (unit(hidden)[0] * V.GN[s, 0:1]).astype(BF)
        V.N1[s] = n1
        recv("qw%d" % s, V.QW.at[s])
        V.QT[s] = nt(V.QW[s], n1).astype(BF)
        recv("tb%d" % s, V.TB.at[s])
        for h in range(3):
            table = jnp.broadcast_to(V.TB[s, h], (8, 32))
            high = table.astype(BF)
            mid = (table - high.astype(F32)).astype(BF)
            low = (table - high.astype(F32) - mid.astype(F32)).astype(BF)
            by_dist = nn(high, back_hot) + nn(mid, back_hot) + nn(low, back_hot)
            bias = row_roll(jnp.broadcast_to(by_dist[0:1], (T, T)), True)
            q = V.QT[s, 64 * h : 64 * h + 64]
            k = V.QT[s, 192 + 64 * h : 256 + 64 * h]
            v = V.QT[s, 384 + 64 * h : 448 + 64 * h]
            score = jnp.where(allowed, tn(q, k) * SCALE + bias, NEG)
            top = jnp.max(score, axis=-1, keepdims=True)
            w = jnp.exp(score - top)
            w = w / jnp.sum(w, axis=-1, keepdims=True)
            V.PS[s, h] = w
            V.OG[s, pl.ds(pl.multiple_of(192 * r + 64 * h, 64), 64)] = nt(
                v, w.astype(BF)
            ).astype(BF)
        mine = V.OG.at[s, pl.ds(pl.multiple_of(192 * r, 192), 192)]
        x_send(lambda peer: mine, mine, "og%d" % s)
        later("og%d" % s, V.OG.at[s, pl.ds(0, 576)])
        if s == 0:
            one_hots(0)
            one_hots(1)
            recv("hb1", V.HB.at[1])
            g = V.HB[1]
            spread(1, jnp.concatenate([g, g], axis=0), V.DS.at[1])
            e_out(V.DS.at[1], V.DR.at[1], "d1")
        mix_end(s)
        recv("og%d" % s, V.OG.at[s, pl.ds(0, 576)])
        middle = hidden + tn(V.OG[s], V.MIX[s])
        V.M[s] = middle
        n2 = (unit(middle)[0] * V.GN[s, 1:2]).astype(BF)
        V.N2[s] = n2
        square = row_sums(middle * middle)
        V.R2[s] = lax.rsqrt(square[0:1] * (1.0 / D) + EPS)

    def spread(s, pair, dst):
        dst[:, 0:D] = nn(V.HH[s, 0], pair).astype(BF)
        extra = nn(V.HH[s, 1], pair[:, 0:256])
        extra += nn(V.HH[s, 2], pair[:, 256:512])
        extra += nn(V.HH[s, 3], pair[:, 512:768])
        dst[:, D:1024] = extra.astype(BF)

    def gather(s, src):
        last = src[:, D:1024]
        return [
            tn(V.HH[s, 0], src[:, 256 * j : 256 * j + 256]) + tn(V.HH[s, 1 + j], last)
            for j in range(3)
        ]

    def gates(s):
        logits = nt(V.N2[s], V.RT[s])
        w = jnp.exp(logits - jnp.max(logits, axis=-1, keepdims=True))
        w = w / jnp.sum(w, axis=-1, keepdims=True)
        V.PR[s] = w
        lane = iota((T, NE), 1).astype(F32)
        for k in range(2):
            col = V.TC[:, 8 + 8 * s + k : 9 + 8 * s + k]
            V.GT[s, :, k : k + 1] = jnp.sum(
                jnp.where(lane == col, w, 0.0), axis=-1, keepdims=True
            )

    def gate_rows(s):
        highs = lows = None
        for k in range(2):
            gate = V.GT[s, :, k : k + 1]
            col = V.TC[:, 24 + 8 * s + k : 25 + 8 * s + k]
            slot_hot = iota((T, 256), 1).astype(F32) == col
            mine = (iota((NE, T), 0) == V.RO[s, k : k + 1]).astype(F32).astype(BF)
            high = gate.astype(BF).astype(F32)
            a = nn(mine, jnp.where(slot_hot, high, 0.0).astype(BF))
            b = nn(mine, jnp.where(slot_hot, gate - high, 0.0).astype(BF))
            highs = a if highs is None else highs + a
            lows = b if lows is None else lows + b
        rows, cols = iota((256, NE), 0), iota((256, NE), 1)
        at12 = (rows == 16 * cols + 12).astype(F32).astype(BF)
        at13 = (rows == 16 * cols + 13).astype(F32).astype(BF)
        return (nn(at12, highs.astype(BF)) + nn(at13, lows.astype(BF))).astype(BF)

    def gate_column(g):
        row, col = iota((HALF, 128), 0), iota((HALF, 128), 1)
        block = jnp.where(row < 128, row // 16, (row - 128) // 4)
        pick = ((col == 16 * block + 12) | (col == 16 * block + 13)).astype(F32).astype(BF)
        spread_gates = nn(pick, V.XR[1, 128 * g : 128 * g + 128, D:1024])
        row, lane = iota((HALF, 256), 0), iota((HALF, 256), 1)
        slot = jnp.where(row < 128, row & 15, 16 + (row & 3))
        return jnp.sum(jnp.where(lane == slot, spread_gates, 0.0), axis=-1, keepdims=True)

    def send_x(s):
        n2 = V.N2[s]
        spread(s, jnp.concatenate([n2, n2], axis=0), V.XS.at[s])
        if s == 1:
            V.XS[s, :, D:1024] = V.XS[s, :, D:1024] + gate_rows(s)
        e_out(V.XS.at[s], V.XR.at[s], "x%d" % s)

    def send_dy(s, g_ref):
        g = g_ref[...].astype(F32)
        pair = [(V.GT[s, :, k : k + 1] * g).astype(BF) for k in range(2)]
        spread(s, jnp.concatenate(pair, axis=0), V.DS.at[s])
        e_out(V.DS.at[s], V.DR.at[s], "d%d" % s)

    q_row, q_col = iota((32, 128), 0), iota((32, 128), 1)
    picks = [
        (q_col == (q_row // 4) * 16 + 4 * j + (q_row & 3)).astype(F32).astype(BF) for j in range(3)
    ]

    def unpack(src, dst, g):
        rows, at = slice(128 * g, 128 * g + 128), HALF * g
        dst[at : at + 128] = src[rows, 0:D]
        for j in range(3):
            dst[at + 128 : at + HALF, 256 * j : 256 * j + 256] = nn(
                picks[j], src[rows, D:1024]
            ).astype(BF)

    def pack(value, dst, g):
        rows = slice(128 * g, 128 * g + 128)
        dst[rows, 0:D] = value[0:128].astype(BF)
        extra = tn(picks[0], value[128:HALF, 0:256].astype(BF))
        extra += tn(picks[1], value[128:HALF, 256:512].astype(BF))
        extra += tn(picks[2], value[128:HALF, 512:768].astype(BF))
        dst[rows, D:1024] = extra.astype(BF)

    def expert_forward(s):
        for g in range(2):
            rows = slice(HALF * g, HALF * g + HALF)
            e_half(V.XR.at[s], "x%d" % s, g)
            unpack(V.XR.at[s], V.XB.at[s], g)
            v = nn(V.XB[s, rows], V.EI[s])
            v2 = v * v
            th = jnp.tanh(0.7978845608028654 * (v + 0.044715 * v * v2))
            V.AB[s, rows] = (0.5 * v * (1.0 + th)).astype(BF)
            V.GD[s, rows] = 0.5 * (1.0 + th) + 0.5 * v * (1.0 - th * th) * (
                0.7978845608028654 * (1.0 + 3.0 * 0.044715 * v2)
            )
            pack(nn(V.AB[s, rows], V.EO[s]), V.YS.at[s], g)
            e_back(V.YS.at[s], V.YR.at[s], "y%d" % s, g)

    def expert_backward(s):
        for g in range(2):
            rows = slice(HALF * g, HALF * g + HALF)
            e_half(V.DR.at[s], "d%d" % s, g)
            unpack(V.DR.at[s], V.DY, g)
            if s == 1:
                V.DY[rows] = (V.DY[rows].astype(F32) * gate_column(g)).astype(BF)
            V.DU[rows] = (nt(V.DY[rows], V.EO[s]) * V.GD[s, rows]).astype(BF)
            pack(nt(V.DU[rows], V.EI[s]), V.ZS.at[s], g)
            e_back(V.ZS.at[s], V.ZR.at[s], "z%d" % s, g)
        if s == 0:
            pl.when(c == 1)(lambda: (reduce_send(1, 0), reduce_send(1, 1)) and None)
        V.EG[s, 1] = tn(V.AB[s], V.DY[...]).astype(BF)
        V.EG[s, 0] = tn(V.XB[s], V.DU[...]).astype(BF)

        @pl.when(c != s)
        def _():
            remote(V.EG.at[s], V.EGR, "eg", mate)

    def tok_send(buf, dst, s, name):
        x_send(
            lambda peer: buf.at[s, pl.ds(pl.multiple_of(TR * peer, TR), TR)],
            dst.at[s, r],
            name + str(s),
        )
        later(name + str(s), buf.at[s, pl.ds(0, 3 * TR)])
        dst[s, r] = buf[s, own_rows]

    def tok_recv(dst, s, name):
        recv(name + str(s), dst.at[s, pl.ds(0, 3)])
        total = dst[s, 0].astype(F32)
        for k in range(1, NX):
            total += dst[s, k].astype(F32)
        return total

    def tok_share(value, ref, name):
        ref[own_rows] = value
        mine = ref.at[own_rows]
        x_send(lambda peer: mine, mine, name)
        later(name, ref.at[pl.ds(0, 3 * TR)])

    def combine(s):
        e_recv(V.YR.at[s], 16, "y%d" % s)
        parts = gather(s, V.YR.at[s])
        g0, g1 = V.GT[s, :, 0:1], V.GT[s, :, 1:2]
        for j in range(3):
            lanes = slice(256 * j, 256 * j + 256)
            V.PK[s, :, lanes] = parts[j].astype(BF)
            V.US[s, :, lanes] = (g0 * parts[j][0:T] + g1 * parts[j][T:]).astype(BF)

    def send_out(s):
        tok_send(V.US, V.UR, s, "u")

    def finish_out(s, ref):
        out = V.M[s, own_rows] + tok_recv(V.UR, s, "u")
        tok_share(out.astype(BF), ref, "h%d" % s)

    def token_grads(s, g_ref):
        g = g_ref[...].astype(F32)
        lane = iota((T, T), 1)
        picked = V.PK[s]
        d0 = jnp.sum(g * picked[0:T].astype(F32), axis=-1, keepdims=True)
        d1 = jnp.sum(g * picked[T:].astype(F32), axis=-1, keepdims=True)
        V.VS[s, :, D:896] = jnp.where(lane == 0, d0, jnp.where(lane == 1, d1, 0.0)).astype(BF)
        own_mix = V.MIX[s, pl.ds(pl.multiple_of(192 * r, 192), 192)]
        gain = V.GN[s, 1:2]
        u2, _ = unit(V.M[s])
        V.GM[...] = nt(own_mix, g_ref[...])
        V.UM[...] = nt(own_mix, u2.astype(BF))
        pr = V.PR[s]
        slim = iota((T, NE), 1).astype(F32)
        dpr = jnp.where(slim == V.TC[:, 8 + 8 * s : 9 + 8 * s], d0, 0.0)
        dpr += jnp.where(slim == V.TC[:, 9 + 8 * s : 10 + 8 * s], d1, 0.0)
        dl = (pr * (dpr - jnp.sum(pr * dpr, axis=-1, keepdims=True))).astype(BF)
        from_router = nn(dl, V.RT[s])
        e_recv(V.ZR.at[s], 16, "z%d" % s)
        parts = gather(s, V.ZR.at[s])
        rows = [parts[j][0:T] + parts[j][T:] for j in range(3)]
        for j in range(3):
            V.VS[s, :, 256 * j : 256 * j + 256] = rows[j].astype(BF)
        du = (jnp.concatenate(rows, axis=1) + from_router) * gain
        heads = nt(V.MIX[s], du.astype(BF))
        dot_u = row_sums(du * u2)
        high = dot_u.astype(BF).astype(F32)
        dot_rows = jnp.where(iota((16, T), 0) == 0, high, dot_u - high).astype(BF)
        for k in range(NX):
            V.QS[s, 208 * k : 208 * k + 192] = heads[192 * k : 192 * k + 192].astype(BF)
            V.QS[s, 208 * k + 192 : 208 * k + 208] = dot_rows
        x_send(
            lambda peer: V.QS.at[s, pl.ds(pl.multiple_of(208 * peer, 16), 208)],
            V.QR.at[s, r],
            "q%d" % s,
        )
        later("q%d" % s, V.QS.at[s, pl.ds(0, 624)])
        V.QR[s, r] = V.QS[s, pl.ds(pl.multiple_of(208 * r, 16), 208)]
        tok_send(V.VS, V.VR, s, "v")

    def middle_grads(s, g_ref):
        total = tok_recv(V.VR, s, "v")
        gain = V.GN[s, 1:2]
        u2, r2 = unit(V.M[s, own_rows])
        pr = V.PR[s, own_rows]
        lane = iota((TR, NE), 1).astype(F32)
        cols = V.TC[own_rows]
        dpr = jnp.where(lane == cols[:, 8 + 8 * s : 9 + 8 * s], total[:, D : D + 1], 0.0)
        dpr += jnp.where(lane == cols[:, 9 + 8 * s : 10 + 8 * s], total[:, D + 1 : D + 2], 0.0)
        dl = (pr * (dpr - jnp.sum(pr * dpr, axis=-1, keepdims=True))).astype(BF)
        dn2 = total[:, 0:D] + nn(dl, V.RT[s])
        du = dn2 * gain
        dm = g_ref[own_rows].astype(F32) + r2 * (
            du - u2 * jnp.mean(du * u2, axis=-1, keepdims=True)
        )
        V.DM[s] = dm
        tok_share(dm.astype(BF), V.DMB.at[s], "m%d" % s)
        V.SM[s, 0:16] = tn(dl, V.N2[s, own_rows])
        V.SM[s, 17:18] = jnp.sum(dn2 * u2, axis=0, keepdims=True)

    def attend_backward(s, h_ref):
        hidden = h_ref[...].astype(F32)
        recv("q%d" % s, V.QR.at[s, pl.ds(0, 3)])
        total = V.QR[s, 0].astype(F32)
        for k in range(1, NX):
            total += V.QR[s, k].astype(F32)
        dot_u = total[192:193] + total[193:194]
        r2 = V.R2[s]
        do = V.GM[...] + r2 * total[0:192] - (r2 * dot_u * (1.0 / D)) * V.UM[...]
        do = do.astype(BF)
        for h in range(3):
            q = V.QT[s, 64 * h : 64 * h + 64]
            k = V.QT[s, 192 + 64 * h : 256 + 64 * h]
            v = V.QT[s, 384 + 64 * h : 448 + 64 * h]
            doh = do[64 * h : 64 * h + 64]
            w = V.PS[s, h]
            dw = tn(doh, v)
            dsc = w * (dw - jnp.sum(w * dw, axis=-1, keepdims=True))
            low = dsc.astype(BF)
            V.DQ[s, 64 * h : 64 * h + 64] = (nt(k, low) * SCALE).astype(BF)
            V.DQ[s, 192 + 64 * h : 256 + 64 * h] = (nn(q, low) * SCALE).astype(BF)
            V.DQ[s, 384 + 64 * h : 448 + 64 * h] = nn(doh, w.astype(BF)).astype(BF)
            V.SC[h] = dsc
        dn1 = tn(V.DQ[s], V.QW[s])
        V.WS[s] = dn1.astype(BF)
        tok_send(V.WS, V.WR, s, "w")
        V.SM[s, 16:32] = jnp.zeros((16, D), F32)
        V.SM[s, 16:17] = jnp.sum(dn1 * unit(hidden)[0], axis=0, keepdims=True)

    def weight_grads(s, part):
        if part == 0:
            V.G16[s, 0:576] = nn(V.DQ[s], V.N1[s]).astype(BF)
            pl.when(c != s)(
                lambda: remote(V.G16.at[s, pl.ds(0, 576)], V.GP.at[pl.ds(0, 576)], "gq", mate)
            )
            return
        for h in range(3):
            turned = jnp.sum(row_roll(V.SC[h], False), axis=0, keepdims=True)
            turned = jnp.sum(
                jnp.broadcast_to(turned, (32, T)) * back_hot.astype(F32), axis=-1, keepdims=True
            )
            spot = (iota((32, T), 0) == iota((32, T), 1)).astype(F32)
            V.SM[s, 18 + h : 19 + h, 0:T] = jnp.sum(turned * spot, axis=0, keepdims=True)
        recv("m%d" % s, V.DMB.at[s, pl.ds(0, 3 * TR)])
        V.G16[s, 576:768] = nn(
            V.OG[s, pl.ds(pl.multiple_of(192 * r, 192), 192)], V.DMB[s]
        ).astype(BF)

        @pl.when(c != s)
        def _():
            remote(V.G16.at[s, pl.ds(576, 192)], V.GP.at[pl.ds(576, 192)], "gp", mate)
            remote(V.SM.at[s], V.SP, "sp", mate)

    def finish_hidden(s, h_ref, ref):
        dn1 = tok_recv(V.WR, s, "w")
        u1, r1 = unit(h_ref[own_rows].astype(F32))
        du = dn1 * V.GN[s, 0:1]
        dh = V.DM[s] + r1 * (du - u1 * jnp.mean(du * u1, axis=-1, keepdims=True))
        tok_share(dh.astype(BF), ref, "g%d" % s)

    h0, g1 = V.HB.at[0], V.HB.at[1]
    recv("hb0", h0)
    attend(0, h0)
    recv("rt0", V.RT.at[0])

    @pl.when(c == 1)
    def _():
        mix_start(1)

    send_x(0)
    gates(0)
    recv("ei0", V.EI.at[0])
    recv("eo0", V.EO.at[0])
    expert_forward(0)
    combine(0)
    send_out(0)
    finish_out(0, V.HX)
    recv("h0", V.HX.at[pl.ds(0, 3 * TR)])

    attend(1, V.HX)
    recv("rt1", V.RT.at[1])
    gates(1)
    send_x(1)
    recv("ei1", V.EI.at[1])
    recv("eo1", V.EO.at[1])
    expert_forward(1)
    expert_backward(1)
    combine(1)
    token_grads(1, g1)
    send_out(1)
    attend_backward(1, V.HX)
    middle_grads(1, g1)
    finish_out(1, V.OUTB.at[1])
    finish_hidden(1, V.HX, V.GG)
    weight_grads(1, 0)
    weight_grads(1, 1)
    recv("g1", V.GG.at[pl.ds(0, 3 * TR)])

    def e_share(ref, rows, name):
        mine = ref.at[rows]

        def step(d, carry):
            remote(mine, mine, name, (c, lax.rem(e + d, NE), r))
            return carry

        lax.fori_loop(1, NE, step, 0)

    gather_rows = pl.ds(pl.multiple_of(48 * e, 48), 48)
    unit_rows = pl.ds(pl.multiple_of(16 * e, 16), 16)

    def reduce_pair(s, part):
        rows = slice(576, 768) if part else slice(0, 576)
        recv("gp" if part else "gq", V.GP.at[pl.ds(rows.start, rows.stop - rows.start)])
        V.GS[rows] = (V.G16[s, rows].astype(F32) + V.GP[rows].astype(F32)).astype(BF)
        if part == 0:
            return
        recv("sp", V.SP)
        small = V.SM[s] + V.SP[...]
        V.SU[...] = jnp.zeros((256, T), F32)
        for j in range(12):
            V.SU[16 * j : 16 * j + 16] = small[
                16 * (j // 6) : 16 * (j // 6) + 16, T * (j % 6) : T * (j % 6) + T
            ]

    def reduce_send(s, part):
        def step(d, carry):
            peer = lax.rem(e + d, NE)

            @pl.when((peer >= 12) if part else (peer < 12))
            def _():
                remote(
                    V.GS.at[pl.ds(pl.multiple_of(peer * 48, 48), 48)],
                    V.GR.at[pl.ds(pl.multiple_of(e * 48, 48), 48)],
                    "gr",
                    (c, peer, r),
                )

            return carry

        lax.fori_loop(1, NE, step, 0)
        if part == 0:
            return
        V.GR[gather_rows] = V.GS[gather_rows]
        e_send(V.SU, V.SR, 16, "sr", False)

    def reduce_sum(s):
        e_recv(V.GR, 48, "gr")
        total = V.GR[0:48].astype(F32)
        for j in range(1, NE):
            total += V.GR[48 * j : 48 * j + 48].astype(F32)
        gf[gather_rows] = total.astype(BF)
        e_share(gf, gather_rows, "gf")
        e_recv(V.SR, 16, "sr")
        tiny = V.SR[0:16]
        for j in range(1, NE):
            tiny += V.SR[16 * j : 16 * j + 16]
        V.XU[r] = tiny
        x_send(lambda peer: V.XU.at[r], V.XU.at[r], "xu")

    def reduce_small(s):
        recv("xu", V.XU.at[pl.ds(0, 3)])
        summed = V.XU[0] + V.XU[1] + V.XU[2] + V.XU[3]
        line = iota((16, T), 0)
        held = (e >= 6) & (line >= 2) & (line <= 4)
        V.SF[unit_rows] = jnp.where(held, V.XU[r], summed)
        e_share(V.SF, unit_rows, "sf")

    send_dy(0, V.GG)
    pl.when(c == 1)(lambda: (reduce_pair(1, 0), reduce_pair(1, 1)) and None)
    expert_backward(0)
    token_grads(0, V.GG)
    attend_backward(0, h0)
    weight_grads(0, 0)
    middle_grads(0, V.GG)

    @pl.when(c == 0)
    def _():
        reduce_pair(0, 0)
        reduce_send(0, 0)

    weight_grads(0, 1)
    pl.when(c == 1)(lambda: reduce_sum(1))

    @pl.when(c == 0)
    def _():
        reduce_pair(0, 1)
        reduce_send(0, 1)

    finish_hidden(0, h0, V.OUTB.at[0])
    pl.when(c == 1)(lambda: reduce_small(1))
    recv("g0", V.OUTB.at[0, pl.ds(0, 3 * TR)])
    recv("h1", V.OUTB.at[1, pl.ds(0, 3 * TR)])
    remote(V.OUTB.at[1 - c], bo.at[c], "bo", mate)
    later("bo", V.OUTB.at[0])
    pltpu.make_async_copy(V.OUTB.at[c], bo.at[c], RS.at[sem_id("boo")]).start()
    pltpu.make_async_copy(V.EG.at[c], eg_own, RS.at[sem_id("ego")]).start()
    recv("eg", V.EGR)
    pltpu.make_async_copy(V.EGR, eg_recv, RS.at[sem_id("egc")]).start()

    @pl.when(c == 0)
    def _():
        reduce_sum(0)
        reduce_small(0)

    later("xu", V.XU.at[pl.ds(0, 3)])
    later("gf", gf.at[pl.ds(0, 15 * 48)])
    later("sf", V.SF.at[pl.ds(0, 240)])
    later("gr", V.GS.at[pl.ds(0, 15 * 48)])
    later("sr", V.SU.at[pl.ds(0, 240)])
    recv("sf", V.SF.at[pl.ds(0, 240)])
    for j in range(6):
        lanes = slice(T * j, T * j + T)
        router_o[:, lanes] = V.SF[16 * j : 16 * j + 16]
        gains_o[:, lanes] = V.SF[96 + 16 * j : 98 + 16 * j]
    bias_o[...] = V.SF[98:101]
    recv("gf", gf.at[pl.ds(0, 15 * 48)])
    recv("bo", bo.at[0])
    recv("boo", bo.at[0])
    recv("ego", eg_own)
    recv("egc", eg_recv)
    for name, ref in pending:
        wait_bytes(SS.at[sem_id(name)], ref)
    wait_bytes(SS.at[sem_id("eg")], V.EGR)
    wait_bytes(SS.at[sem_id("gq")], V.GP.at[pl.ds(0, 576)])
    wait_bytes(SS.at[sem_id("gp")], V.GP.at[pl.ds(0, 192)])
    wait_bytes(SS.at[sem_id("sp")], V.SP)
    for s in range(2):
        mix_done(s)


def kernel(*refs):
    ins, outs = refs[:12], refs[12:19]
    V = types.SimpleNamespace(**dict(zip(NAMES, refs[19:])))
    SS, RS = refs[-2:]
    body(ins, outs, V, SS, RS)


N_SEMS = 112


PARTS = 2


def last_kernel(own, got, gf1, gf2, bo, ga, ro, bi, ein, eout, qkv, mix, bo_o, ga_o, ro_o, bi_o):
    ein[...] = own[0].astype(F32) + got[0].astype(F32)
    eout[...] = own[1].astype(F32) + got[1].astype(F32)
    qkv[...] = gf1[...].astype(F32)
    mix[...] = gf2[...].astype(F32)
    bo_o[...] = bo[...]
    ga_o[...] = ga[...]
    ro_o[...] = ro[...]
    for h in range(3):
        bi_o[h] = bi[h : h + 1, 0:32]


def last(own, got, gf, bo, ga, ro, bi):
    shape = jax.ShapeDtypeStruct
    n = D // PARTS

    def whole(x):
        return pl.BlockSpec(x.shape, lambda i: (0,) * len(x.shape))

    both = pl.BlockSpec((2, n, D), lambda i: (0, i, 0))
    line = pl.BlockSpec((n, D), lambda i: (i, 0))
    q_spec = pl.BlockSpec((576 // PARTS, D), lambda i: (i, 0))
    m_spec = pl.BlockSpec((192 // PARTS, D), lambda i: (i, 0))
    return pl.pallas_call(
        last_kernel,
        grid=(PARTS,),
        in_specs=[
            both,
            both,
            q_spec,
            pl.BlockSpec((192 // PARTS, D), lambda i: (3 * PARTS + i, 0)),
            whole(bo),
            whole(ga),
            whole(ro),
            whole(bi),
        ],
        out_specs=[
            line,
            line,
            q_spec,
            m_spec,
            whole(bo),
            whole(ga),
            whole(ro),
            pl.BlockSpec((3, 1, 32), lambda i: (0, 0, 0)),
        ],
        out_shape=[
            shape((D, D), F32),
            shape((D, D), F32),
            shape((576, D), F32),
            shape((192, D), F32),
            shape(bo.shape, bo.dtype),
            shape(ga.shape, ga.dtype),
            shape(ro.shape, ro.dtype),
            shape((3, 1, 32), F32),
        ],
    )(own, got, gf, gf, bo, ga, ro, bi)


def on_device(
    boundary,
    segments,
    buckets,
    routes,
    slots,
    gains,
    qkv_weight,
    mix_weight,
    bias_table,
    router,
    expert_in,
    expert_out,
):
    qkv = jnp.transpose(qkv_weight[0], (1, 2, 0)).reshape(576, D)
    any_space = pl.BlockSpec(memory_space=pl.ANY)
    vmem = pl.BlockSpec(memory_space=pltpu.VMEM)
    shape = jax.ShapeDtypeStruct
    outs = pl.pallas_call(
        kernel,
        out_shape=[
            shape((2, T, D), BF),
            shape((2, D, D), BF),
            shape((2, D, D), BF),
            shape((D, D), BF),
            shape((2, D), F32),
            shape((NE, D), F32),
            shape((3, T), F32),
        ],
        in_specs=[any_space] * 12,
        out_specs=[vmem, any_space, any_space, vmem, vmem, vmem, vmem],
        scratch_shapes=[pltpu.VMEM(*SCRATCH[name]) for name in NAMES]
        + [pltpu.SemaphoreType.DMA((N_SEMS,)), pltpu.SemaphoreType.DMA((N_SEMS,))],
        compiler_params=pltpu.CompilerParams(
            collective_id=0, has_side_effects=True, vmem_limit_bytes=60 * 1024 * 1024
        ),
    )(
        boundary[0],
        segments,
        buckets.reshape(1, T),
        jnp.transpose(routes[0], (0, 2, 1)),
        jnp.transpose(slots[0], (0, 2, 1)),
        gains[0],
        qkv,
        mix_weight[0],
        jnp.transpose(bias_table, (2, 0, 1)),
        jnp.transpose(router[0]),
        expert_in[0, 0],
        expert_out[0, 0],
    )
    bo, eg_own, eg_recv, gf, grad_gains, grad_router, grad_bias = outs
    grad_in, grad_out, grad_qkv, grad_mix, bo, grad_gains, grad_router, grad_bias = last(
        eg_own, eg_recv, gf, bo, grad_gains, grad_router, grad_bias
    )
    return (
        bo[None],
        grad_gains[None],
        jnp.transpose(grad_qkv.reshape(3, 192, D), (2, 0, 1))[None],
        grad_mix[None],
        jnp.transpose(grad_bias, (1, 2, 0)),
        jnp.transpose(grad_router)[None],
        grad_in[None, None],
        grad_out[None, None],
    )


def solution(mesh):
    in_specs = (
        P("section", None, "expert", None),
        P(None, "expert", None),
        P(),
        P("section", None, "expert", None),
        P("section", None, "expert", None),
        P("section", None, None),
        P("section", None, None, "head"),
        P("section", "head", None),
        P("section", None, "head"),
        P("section", None, None),
        P("section", "expert", None, "head"),
        P("section", "expert", "head", None),
    )
    out_specs = (
        P("section", None, "expert", None),
        P("section", None, None),
        P("section", None, None, "head"),
        P("section", "head", None),
        P("section", None, "head"),
        P("section", None, None),
        P("section", "expert", None, "head"),
        P("section", "expert", "head", None),
    )
    return jax.shard_map(
        on_device, mesh=mesh, in_specs=in_specs, out_specs=out_specs, check_vma=False
    )
```

time: 191 us -> 165 us (0.86)
  Pallas kernels: 179 us -> 164 us
  local copies, waits for them, and re-layouts: 6.35 us -> 0 us
  other arithmetic: 5.09 us -> 0 us
    pallas_call x1, Pallas kernels: 179 us -> 159 us  [on_device(): pl.pallas_call(kernel, out_shape=[shape((2, T, D), BF), shape((2, D, D),...]
    pallas_call x0 -> x1, Pallas kernels: none -> 5.17 us  [last(): pl.pallas_call(last_kernel, grid=(PARTS,), in_specs=[both, both, q_spec,...]
    unnamed x15 -> x0, local copies, waits for them, and re-layouts: 3.81 us -> none
    add x1 -> x0, other arithmetic: 2.89 us -> none  [on_device(): grad_expert = eg_own.astype(F32) + eg_recv.astype(F32)]
    another operation x1 -> x0, local copies, waits for them, and re-layouts: 2.49 us -> none  [on_device(): grad_expert[1][None, None]]
    broadcast_in_dim x2 -> x0, other arithmetic: 2.2 us -> none  [the longest x1 1.35 us: on_device(): grad_qkv[None]]
where the time goes in v2:
time: 165 us
  Pallas kernels  164 us (99%)
    pallas_call x1, Pallas kernels, on_device(): pl.pallas_call(kernel, out_shape=[shape((2, T, D), BF), shape((2, D, D),...  159 us
    pallas_call x1, Pallas kernels, last(): pl.pallas_call(last_kernel, grid=(PARTS,), in_specs=[both, both, q_spec,...  5.17 us

profile of v2, /device:TPU:0, one launch (start us, length us, event | category | flops | bytes accessed | tf_op | source)
XLA Modules:
  0.0 164.9 jit_solution(6831172127191732203)
XLA Ops:
  0.6 159.0 %shard_map.179 = (bf16[2,128,768]{2,1,0:T(8,128)(2,1)}, bf16[2,768,768]{2,1,0:T(8,128)(2,1)}, bf16[2,768,768]{2,1,0:T(8,128)(2,1)}, bf16[768,768]{1,0:T(8,128)(2...) custom-call(bf16[2,128,768]{2,1,0:T(8,128)(2,1)} %bitcast.38, s32[2,1,128]{2,1,0:T(1,128)} %refs_1_.1, ...), custom_call_target="tpu_custom_call" | custom-call | tf_op jit(solution)/shard_map/pallas_call | solution.py:911
  159.6 5.2 %shard_map.180 = (f32[768,768]{1,0:T(8,128)}, f32[768,768]{1,0:T(8,128)}, f32[576,768]{1,0:T(8,128)}, f32[192,768]{1,0:T(8,128)}, bf16[2,128,768]{2,1,0:T(8,128)...) custom-call(bf16[2,768,768]{2,1,0:T(8,128)(2,1)} %get-tuple-element.23.own, ...), custom_call_target="tpu_custom_call" | custom-call | tf_op jit(solution)/shard_map/pallas_call | solution.py:857

commit v3 on v2

--- a/solution.py
+++ b/solution.py
@@ -115,8 +115,10 @@
     OUTB=((2, T, D), BF),
     EG=((2, 2, D, D), BF),
     EGR=((2, D, D), BF),
-    G16=((2, D, D), BF),
-    GP=((D, D), BF),
+    NP=((T, D), BF),
+    OP=((192, T), BF),
+    DP=((576, T), BF),
+    MP=((T, D), BF),
     GS=((D, D), BF),
     GR=((D, D), BF),
     SM=((2, 32, D), F32),
@@ -189,6 +191,20 @@
         pltpu.make_async_copy(own_src, buf.at[c], RS.at[k0 + c]).start()
         later(name + "0", buf.at[0])
 
+    def x_send(src, dst, name):
+        for d in range(1, NX):
+            peer = lax.rem(r + d, NX)
+            remote(src(peer), dst, name, (c, e, peer))
+
+    def mix_start(s):
+        own = V.MIX.at[s, pl.ds(pl.multiple_of(192 * r, 192), 192)]
+        x_send(lambda peer: mx_in, own, "mix%d" % s)
+        pltpu.make_async_copy(mx_in, own, RS.at[sem_id("mixo%d" % s)]).start()
+
+    @pl.when(c == 0)
+    def _():
+        mix_start(0)
+
     share("hb", bnd.at[c], bnd.at[1 - c], V.HB)
     share("gn", gns, gns, V.GN)
     share("qw", qw_in, qw_in, V.QW)
@@ -198,16 +214,6 @@
     share("ro", rts.at[c], rts.at[1 - c], V.RO)
     share("sl", slt.at[c], slt.at[1 - c], V.SL)
 
-    def x_send(src, dst, name):
-        for d in range(1, NX):
-            peer = lax.rem(r + d, NX)
-            remote(src(peer), dst, name, (c, e, peer))
-
-    def mix_start(s):
-        own = V.MIX.at[s, pl.ds(pl.multiple_of(192 * r, 192), 192)]
-        x_send(lambda peer: mx_in, own, "mix%d" % s)
-        pltpu.make_async_copy(mx_in, own, RS.at[sem_id("mixo%d" % s)]).start()
-
     def mix_end(s):
         @pl.when(c == s)
         def _():
@@ -225,13 +231,7 @@
         def _():
             wait_bytes(SS.at[sem_id("mixr%d" % s)], V.MIX.at[s])
 
-    @pl.when(c == 0)
-    def _():
-        mix_start(0)
-
     share("rt", rt_in, rt_in, V.RT)
-    share("ei", ei_in, ei_in, V.EI)
-    share("eo", eo_in, eo_in, V.EO)
 
     def e_send(src, dst, rows, name, note=True):
         def step(d, carry):
@@ -353,6 +353,12 @@
             ).astype(BF)
         mine = V.OG.at[s, pl.ds(pl.multiple_of(192 * r, 192), 192)]
         x_send(lambda peer: mine, mine, "og%d" % s)
+
+        @pl.when(c != s)
+        def _():
+            remote(V.N1.at[s], V.NP, "np", mate)
+            remote(mine, V.OP, "op", mate)
+
         later("og%d" % s, V.OG.at[s, pl.ds(0, 576)])
         if s == 0:
             one_hots(0)
@@ -362,6 +368,9 @@
             spread(1, jnp.concatenate([g, g], axis=0), V.DS.at[1])
             e_out(V.DS.at[1], V.DR.at[1], "d1")
         mix_end(s)
+        if s == 0:
+            share("ei", ei_in, ei_in, V.EI)
+            share("eo", eo_in, eo_in, V.EO)
         recv("og%d" % s, V.OG.at[s, pl.ds(0, 576)])
         middle = hidden + tn(V.OG[s], V.MIX[s])
         V.M[s] = middle
@@ -481,8 +490,6 @@
             V.DU[rows] = (nt(V.DY[rows], V.EO[s]) * V.GD[s, rows]).astype(BF)
             pack(nt(V.DU[rows], V.EI[s]), V.ZS.at[s], g)
             e_back(V.ZS.at[s], V.ZR.at[s], "z%d" % s, g)
-        if s == 0:
-            pl.when(c == 1)(lambda: (reduce_send(1, 0), reduce_send(1, 1)) and None)
         V.EG[s, 1] = tn(V.AB[s], V.DY[...]).astype(BF)
         V.EG[s, 0] = tn(V.XB[s], V.DU[...]).astype(BF)
 
@@ -611,19 +618,14 @@
             V.DQ[s, 192 + 64 * h : 256 + 64 * h] = (nn(q, low) * SCALE).astype(BF)
             V.DQ[s, 384 + 64 * h : 448 + 64 * h] = nn(doh, w.astype(BF)).astype(BF)
             V.SC[h] = dsc
+        pl.when(c != s)(lambda: remote(V.DQ.at[s], V.DP, "dp", mate))
         dn1 = tn(V.DQ[s], V.QW[s])
         V.WS[s] = dn1.astype(BF)
         tok_send(V.WS, V.WR, s, "w")
         V.SM[s, 16:32] = jnp.zeros((16, D), F32)
         V.SM[s, 16:17] = jnp.sum(dn1 * unit(hidden)[0], axis=0, keepdims=True)
 
-    def weight_grads(s, part):
-        if part == 0:
-            V.G16[s, 0:576] = nn(V.DQ[s], V.N1[s]).astype(BF)
-            pl.when(c != s)(
-                lambda: remote(V.G16.at[s, pl.ds(0, 576)], V.GP.at[pl.ds(0, 576)], "gq", mate)
-            )
-            return
+    def small_grads(s):
         for h in range(3):
             turned = jnp.sum(row_roll(V.SC[h], False), axis=0, keepdims=True)
             turned = jnp.sum(
@@ -632,13 +634,10 @@
             spot = (iota((32, T), 0) == iota((32, T), 1)).astype(F32)
             V.SM[s, 18 + h : 19 + h, 0:T] = jnp.sum(turned * spot, axis=0, keepdims=True)
         recv("m%d" % s, V.DMB.at[s, pl.ds(0, 3 * TR)])
-        V.G16[s, 576:768] = nn(
-            V.OG[s, pl.ds(pl.multiple_of(192 * r, 192), 192)], V.DMB[s]
-        ).astype(BF)
 
         @pl.when(c != s)
         def _():
-            remote(V.G16.at[s, pl.ds(576, 192)], V.GP.at[pl.ds(576, 192)], "gp", mate)
+            remote(V.DMB.at[s], V.MP, "mp", mate)
             remote(V.SM.at[s], V.SP, "sp", mate)
 
     def finish_hidden(s, h_ref, ref):
@@ -647,6 +646,85 @@
         du = dn1 * V.GN[s, 0:1]
         dh = V.DM[s] + r1 * (du - u1 * jnp.mean(du * u1, axis=-1, keepdims=True))
         tok_share(dh.astype(BF), ref, "g%d" % s)
+
+    def e_share(ref, at, name):
+        mine = ref.at[at]
+
+        def step(d, carry):
+            remote(mine, mine, name, (c, lax.rem(e + d, NE), r))
+            return carry
+
+        lax.fori_loop(1, NE, step, 0)
+
+    gather_rows = pl.ds(pl.multiple_of(48 * e, 48), 48)
+    unit_rows = pl.ds(pl.multiple_of(16 * e, 16), 16)
+    halves = [pl.ds(0, 384), pl.ds(384, 384)]
+
+    def reduce_send(part):
+        for h in range(2):
+
+            def step(d, carry):
+                peer = lax.rem(e + d, NE)
+
+                @pl.when((peer >= 12) if part else (peer < 12))
+                def _():
+                    remote(
+                        V.GS.at[pl.ds(pl.multiple_of(peer * 48, 48), 48), halves[h]],
+                        V.GR.at[gather_rows, halves[h]],
+                        "gr" + "ab"[h],
+                        (c, peer, r),
+                    )
+
+                return carry
+
+            lax.fori_loop(1, NE, step, 0)
+
+    def reduce_first(s):
+        recv("np", V.NP)
+        recv("dp", V.DP)
+        V.GS[0:576] = (nn(V.DQ[s], V.N1[s]) + nn(V.DP[...], V.NP[...])).astype(BF)
+        reduce_send(0)
+
+    def reduce_second(s):
+        recv("op", V.OP)
+        recv("mp", V.MP)
+        own = V.OG[s, pl.ds(pl.multiple_of(192 * r, 192), 192)]
+        V.GS[576:768] = (nn(own, V.DMB[s]) + nn(V.OP[...], V.MP[...])).astype(BF)
+        reduce_send(1)
+        V.GR[gather_rows] = V.GS[gather_rows]
+        recv("sp", V.SP)
+        small = V.SM[s] + V.SP[...]
+        V.SU[...] = jnp.zeros((256, T), F32)
+        for j in range(12):
+            V.SU[16 * j : 16 * j + 16] = small[
+                16 * (j // 6) : 16 * (j // 6) + 16, T * (j % 6) : T * (j % 6) + T
+            ]
+        e_send(V.SU, V.SR, 16, "sr", False)
+
+    def reduce_sum(s):
+        for h in range(2):
+            recv("gr" + "ab"[h], V.GR.at[pl.ds(0, 720), halves[h]])
+            cols = slice(384 * h, 384 * h + 384)
+            total = V.GR[0:48, cols].astype(F32)
+            for j in range(1, NE):
+                total += V.GR[48 * j : 48 * j + 48, cols].astype(F32)
+            gf[gather_rows, cols] = total.astype(BF)
+            e_share(gf, (gather_rows, halves[h]), "gf" + "ab"[h])
+            if h == 0:
+                e_recv(V.SR, 16, "sr")
+                tiny = V.SR[0:16]
+                for j in range(1, NE):
+                    tiny += V.SR[16 * j : 16 * j + 16]
+                V.XU[r] = tiny
+                x_send(lambda peer: V.XU.at[r], V.XU.at[r], "xu")
+
+    def reduce_small(s):
+        recv("xu", V.XU.at[pl.ds(0, 3)])
+        summed = V.XU[0] + V.XU[1] + V.XU[2] + V.XU[3]
+        line = iota((16, T), 0)
+        held = (e >= 6) & (line >= 2) & (line <= 4)
+        V.SF[unit_rows] = jnp.where(held, V.XU[r], summed)
+        e_share(V.SF, unit_rows, "sf")
 
     h0, g1 = V.HB.at[0], V.HB.at[1]
     recv("hb0", h0)
@@ -679,103 +757,23 @@
     token_grads(1, g1)
     send_out(1)
     attend_backward(1, V.HX)
+    pl.when(c == 1)(lambda: reduce_first(1))
     middle_grads(1, g1)
     finish_out(1, V.OUTB.at[1])
     finish_hidden(1, V.HX, V.GG)
-    weight_grads(1, 0)
-    weight_grads(1, 1)
+    small_grads(1)
     recv("g1", V.GG.at[pl.ds(0, 3 * TR)])
 
-    def e_share(ref, rows, name):
-        mine = ref.at[rows]
-
-        def step(d, carry):
-            remote(mine, mine, name, (c, lax.rem(e + d, NE), r))
-            return carry
-
-        lax.fori_loop(1, NE, step, 0)
-
-    gather_rows = pl.ds(pl.multiple_of(48 * e, 48), 48)
-    unit_rows = pl.ds(pl.multiple_of(16 * e, 16), 16)
-
-    def reduce_pair(s, part):
-        rows = slice(576, 768) if part else slice(0, 576)
-        recv("gp" if part else "gq", V.GP.at[pl.ds(rows.start, rows.stop - rows.start)])
-        V.GS[rows] = (V.G16[s, rows].astype(F32) + V.GP[rows].astype(F32)).astype(BF)
-        if part == 0:
-            return
-        recv("sp", V.SP)
-        small = V.SM[s] + V.SP[...]
-        V.SU[...] = jnp.zeros((256, T), F32)
-        for j in range(12):
-            V.SU[16 * j : 16 * j + 16] = small[
-                16 * (j // 6) : 16 * (j // 6) + 16, T * (j % 6) : T * (j % 6) + T
-            ]
-
-    def reduce_send(s, part):
-        def step(d, carry):
-            peer = lax.rem(e + d, NE)
-
-            @pl.when((peer >= 12) if part else (peer < 12))
-            def _():
-                remote(
-                    V.GS.at[pl.ds(pl.multiple_of(peer * 48, 48), 48)],
-                    V.GR.at[pl.ds(pl.multiple_of(e * 48, 48), 48)],
-                    "gr",
-                    (c, peer, r),
-                )
-
-            return carry
-
-        lax.fori_loop(1, NE, step, 0)
-        if part == 0:
-            return
-        V.GR[gather_rows] = V.GS[gather_rows]
-        e_send(V.SU, V.SR, 16, "sr", False)
-
-    def reduce_sum(s):
-        e_recv(V.GR, 48, "gr")
-        total = V.GR[0:48].astype(F32)
-        for j in range(1, NE):
-            total += V.GR[48 * j : 48 * j + 48].astype(F32)
-        gf[gather_rows] = total.astype(BF)
-        e_share(gf, gather_rows, "gf")
-        e_recv(V.SR, 16, "sr")
-        tiny = V.SR[0:16]
-        for j in range(1, NE):
-            tiny += V.SR[16 * j : 16 * j + 16]
-        V.XU[r] = tiny
-        x_send(lambda peer: V.XU.at[r], V.XU.at[r], "xu")
-
-    def reduce_small(s):
-        recv("xu", V.XU.at[pl.ds(0, 3)])
-        summed = V.XU[0] + V.XU[1] + V.XU[2] + V.XU[3]
-        line = iota((16, T), 0)
-        held = (e >= 6) & (line >= 2) & (line <= 4)
-        V.SF[unit_rows] = jnp.where(held, V.XU[r], summed)
-        e_share(V.SF, unit_rows, "sf")
-
     send_dy(0, V.GG)
-    pl.when(c == 1)(lambda: (reduce_pair(1, 0), reduce_pair(1, 1)) and None)
+    pl.when(c == 1)(lambda: reduce_second(1))
     expert_backward(0)
     token_grads(0, V.GG)
     attend_backward(0, h0)
-    weight_grads(0, 0)
+    pl.when(c == 1)(lambda: reduce_sum(1))
+    pl.when(c == 0)(lambda: reduce_first(0))
     middle_grads(0, V.GG)
-
-    @pl.when(c == 0)
-    def _():
-        reduce_pair(0, 0)
-        reduce_send(0, 0)
-
-    weight_grads(0, 1)
-    pl.when(c == 1)(lambda: reduce_sum(1))
-
-    @pl.when(c == 0)
-    def _():
-        reduce_pair(0, 1)
-        reduce_send(0, 1)
-
+    small_grads(0)
+    pl.when(c == 0)(lambda: reduce_second(0))
     finish_hidden(0, h0, V.OUTB.at[0])
     pl.when(c == 1)(lambda: reduce_small(1))
     recv("g0", V.OUTB.at[0, pl.ds(0, 3 * TR)])
@@ -793,9 +791,10 @@
         reduce_small(0)
 
     later("xu", V.XU.at[pl.ds(0, 3)])
-    later("gf", gf.at[pl.ds(0, 15 * 48)])
+    for h in range(2):
+        later("gf" + "ab"[h], gf.at[pl.ds(0, 720), halves[h]])
+        later("gr" + "ab"[h], V.GS.at[pl.ds(0, 720), halves[h]])
     later("sf", V.SF.at[pl.ds(0, 240)])
-    later("gr", V.GS.at[pl.ds(0, 15 * 48)])
     later("sr", V.SU.at[pl.ds(0, 240)])
     recv("sf", V.SF.at[pl.ds(0, 240)])
     for j in range(6):
@@ -803,7 +802,8 @@
         router_o[:, lanes] = V.SF[16 * j : 16 * j + 16]
         gains_o[:, lanes] = V.SF[96 + 16 * j : 98 + 16 * j]
     bias_o[...] = V.SF[98:101]
-    recv("gf", gf.at[pl.ds(0, 15 * 48)])
+    for h in range(2):
+        recv("gf" + "ab"[h], gf.at[pl.ds(0, 720), halves[h]])
     recv("bo", bo.at[0])
     recv("boo", bo.at[0])
     recv("ego", eg_own)
@@ -811,8 +811,10 @@
     for name, ref in pending:
         wait_bytes(SS.at[sem_id(name)], ref)
     wait_bytes(SS.at[sem_id("eg")], V.EGR)
-    wait_bytes(SS.at[sem_id("gq")], V.GP.at[pl.ds(0, 576)])
-    wait_bytes(SS.at[sem_id("gp")], V.GP.at[pl.ds(0, 192)])
+    wait_bytes(SS.at[sem_id("np")], V.NP)
+    wait_bytes(SS.at[sem_id("op")], V.OP)
+    wait_bytes(SS.at[sem_id("dp")], V.DP)
+    wait_bytes(SS.at[sem_id("mp")], V.MP)
     wait_bytes(SS.at[sem_id("sp")], V.SP)
     for s in range(2):
         mix_done(s)

time: 165 us -> 164 us (level)
  no operation moved by 1% of the time
where the time goes in v3:
time: 164 us; the launch traced here: 163 us
  Pallas kernels  163 us (99%)
    pallas_call x1, Pallas kernels, on_device(): pl.pallas_call(kernel, out_shape=[shape((2, T, D), BF), shape((2, D, D),...  158 us
    pallas_call x1, Pallas kernels, last(): pl.pallas_call(last_kernel, grid=(PARTS,), in_specs=[both, both, q_spec,...  5.17 us

profile of v3, /device:TPU:0, one launch (start us, length us, event | category | flops | bytes accessed | tf_op | source)
XLA Modules:
  0.0 163.5 jit_solution(16966390408218789327)
XLA Ops:
  0.6 157.5 %shard_map.179 = (bf16[2,128,768]{2,1,0:T(8,128)(2,1)}, bf16[2,768,768]{2,1,0:T(8,128)(2,1)}, bf16[2,768,768]{2,1,0:T(8,128)(2,1)}, bf16[768,768]{1,0:T(8,128)(2...) custom-call(bf16[2,128,768]{2,1,0:T(8,128)(2,1)} %bitcast.38, s32[2,1,128]{2,1,0:T(1,128)} %refs_1_.1, ...), custom_call_target="tpu_custom_call" | custom-call | tf_op jit(solution)/shard_map/pallas_call | solution.py:913
  158.2 5.2 %shard_map.180 = (f32[768,768]{1,0:T(8,128)}, f32[768,768]{1,0:T(8,128)}, f32[576,768]{1,0:T(8,128)}, f32[192,768]{1,0:T(8,128)}, bf16[2,128,768]{2,1,0:T(8,128)...) custom-call(bf16[2,768,768]{2,1,0:T(8,128)(2,1)} %get-tuple-element.23.own, ...), custom_call_target="tpu_custom_call" | custom-call | tf_op jit(solution)/shard_map/pallas_call | solution.py:859

commit v4 on v3

--- a/solution.py
+++ b/solution.py
@@ -46,8 +46,8 @@
     return x
 
 
-ORDER = [(0, 0), (0, 1), (0, 3), (1, 0), (3, 0), (1, 1), (3, 3), (1, 3)]
-ORDER += [(3, 1), (0, 2), (2, 0), (1, 2), (3, 2), (2, 1), (2, 3), (2, 2)]
+ORDER = [(0, 0), (2, 2), (2, 1), (1, 2), (2, 3), (3, 2), (0, 2), (2, 0)]
+ORDER += [(1, 1), (3, 3), (1, 3), (3, 1), (0, 1), (0, 3), (1, 0), (3, 0)]
 HALF = 160
 
 SEMS = {}
@@ -192,7 +192,7 @@
         later(name + "0", buf.at[0])
 
     def x_send(src, dst, name):
-        for d in range(1, NX):
+        for d in (2, 1, 3):
             peer = lax.rem(r + d, NX)
             remote(src(peer), dst, name, (c, e, peer))
 

time: 164 us -> 159 us (0.970)
  Pallas kernels: 163 us -> 158 us
    pallas_call x1, Pallas kernels: 158 us -> 153 us  [on_device(): pl.pallas_call(kernel, out_shape=[shape((2, T, D), BF), shape((2, D, D),...]
where the time goes in v4:
time: 159 us
  Pallas kernels  158 us (99%)
    pallas_call x1, Pallas kernels, on_device(): pl.pallas_call(kernel, out_shape=[shape((2, T, D), BF), shape((2, D, D),...  153 us
    pallas_call x1, Pallas kernels, last(): pl.pallas_call(last_kernel, grid=(PARTS,), in_specs=[both, both, q_spec,...  5.17 us

profile of v4, /device:TPU:0, one launch (start us, length us, event | category | flops | bytes accessed | tf_op | source)
XLA Modules:
  0.0 158.8 jit_solution(713656450072695638)
XLA Ops:
  0.6 152.9 %shard_map.179 = (bf16[2,128,768]{2,1,0:T(8,128)(2,1)}, bf16[2,768,768]{2,1,0:T(8,128)(2,1)}, bf16[2,768,768]{2,1,0:T(8,128)(2,1)}, bf16[768,768]{1,0:T(8,128)(2...) custom-call(bf16[2,128,768]{2,1,0:T(8,128)(2,1)} %bitcast.38, s32[2,1,128]{2,1,0:T(1,128)} %refs_1_.1, ...), custom_call_target="tpu_custom_call" | custom-call | tf_op jit(solution)/shard_map/pallas_call | solution.py:913
  153.5 5.2 %shard_map.180 = (f32[768,768]{1,0:T(8,128)}, f32[768,768]{1,0:T(8,128)}, f32[576,768]{1,0:T(8,128)}, f32[192,768]{1,0:T(8,128)}, bf16[2,128,768]{2,1,0:T(8,128)...) custom-call(bf16[2,768,768]{2,1,0:T(8,128)(2,1)} %get-tuple-element.23.own, ...), custom_call_target="tpu_custom_call" | custom-call | tf_op jit(solution)/shard_map/pallas_call | solution.py:859

commit v5 on v4

--- a/solution.py
+++ b/solution.py
@@ -233,9 +233,13 @@
 
     share("rt", rt_in, rt_in, V.RT)
 
+    def for_far(step):
+        for dy, dz in ORDER[1:]:
+            step(lax.rem(e // 4 + dy, 4) * 4 + lax.rem(lax.rem(e, 4) + dz, 4), 0)
+
     def e_send(src, dst, rows, name, note=True):
         def step(d, carry):
-            peer = lax.rem(e + d, NE)
+            peer = d
             remote(
                 src.at[pl.ds(pl.multiple_of(peer * rows, rows), rows)],
                 dst.at[pl.ds(pl.multiple_of(e * rows, rows), rows)],
@@ -244,7 +248,7 @@
             )
             return carry
 
-        lax.fori_loop(1, NE, step, 0)
+        for_far(step)
         if note:
             later(name, src.at[pl.ds(0, (NE - 1) * rows)])
         mine = pl.ds(pl.multiple_of(e * rows, rows), rows)
@@ -651,10 +655,10 @@
         mine = ref.at[at]
 
         def step(d, carry):
-            remote(mine, mine, name, (c, lax.rem(e + d, NE), r))
+            remote(mine, mine, name, (c, d, r))
             return carry
 
-        lax.fori_loop(1, NE, step, 0)
+        for_far(step)
 
     gather_rows = pl.ds(pl.multiple_of(48 * e, 48), 48)
     unit_rows = pl.ds(pl.multiple_of(16 * e, 16), 16)
@@ -664,7 +668,7 @@
         for h in range(2):
 
             def step(d, carry):
-                peer = lax.rem(e + d, NE)
+                peer = d
 
                 @pl.when((peer >= 12) if part else (peer < 12))
                 def _():
@@ -677,7 +681,7 @@
 
                 return carry
 
-            lax.fori_loop(1, NE, step, 0)
+            for_far(step)
 
     def reduce_first(s):
         recv("np", V.NP)

time: 159 us -> 158 us (level)
  no operation moved by 1% of the time
where the time goes in v5:
time: 158 us
  Pallas kernels  157 us (99%)
    pallas_call x1, Pallas kernels, on_device(): pl.pallas_call(kernel, out_shape=[shape((2, T, D), BF), shape((2, D, D),...  152 us
    pallas_call x1, Pallas kernels, last(): pl.pallas_call(last_kernel, grid=(PARTS,), in_specs=[both, both, q_spec,...  5.17 us

profile of v5, /device:TPU:0, one launch (start us, length us, event | category | flops | bytes accessed | tf_op | source)
XLA Modules:
  0.0 157.7 jit_solution(2391476559955264234)
XLA Ops:
  0.6 151.7 %shard_map.179 = (bf16[2,128,768]{2,1,0:T(8,128)(2,1)}, bf16[2,768,768]{2,1,0:T(8,128)(2,1)}, bf16[2,768,768]{2,1,0:T(8,128)(2,1)}, bf16[768,768]{1,0:T(8,128)(2...) custom-call(bf16[2,128,768]{2,1,0:T(8,128)(2,1)} %bitcast.38, s32[2,1,128]{2,1,0:T(1,128)} %refs_1_.1, ...), custom_call_target="tpu_custom_call" | custom-call | tf_op jit(solution)/shard_map/pallas_call | solution.py:917
  152.4 5.2 %shard_map.180 = (f32[768,768]{1,0:T(8,128)}, f32[768,768]{1,0:T(8,128)}, f32[576,768]{1,0:T(8,128)}, f32[192,768]{1,0:T(8,128)}, bf16[2,128,768]{2,1,0:T(8,128)...) custom-call(bf16[2,768,768]{2,1,0:T(8,128)(2,1)} %get-tuple-element.23.own, ...), custom_call_target="tpu_custom_call" | custom-call | tf_op jit(solution)/shard_map/pallas_call | solution.py:863
